TPU v7x, 256 devices: a whole 4x4x8 slice. The times are simulated.
256 devices in a mesh: ctx: 64 (over z, x_hi, y), head: 4 (over x_lo, core).
Axes of the slice: x: 4 (x_hi: 2, x_lo: 2; x = x_hi * 2 + x_lo), y: 4, z: 8, core: 2. Of those that a mesh axis runs over, the one named last changes fastest.
Arguments:
- queries: bfloat16 [16384, 4096], P(('ctx', 'head')), may hold values from -6 to 6
- keys: bfloat16 [16384, 512], P(('ctx', 'head')), may hold values from -6 to 6
- values: bfloat16 [16384, 512], P(('ctx', 'head')), may hold values from -6 to 6
- out_grad: bfloat16 [16384, 4096], P(('ctx', 'head')), may hold values from -6 to 6
- lse: float32 [16384, 32], P('ctx', 'head'), may hold values from 4.5 to 5.5
- delta: float32 [16384, 32], P('ctx', 'head'), may hold values from -15 to 15
- gate_block: int32 [32, 32], replicated, may hold values from 0 to 30, as said below
Outputs:
- grad_queries: bfloat16 [16384, 4096], P(('ctx', 'head'))
- key_gradient: bfloat16 [16384, 512], P(('ctx', 'head'))
- value_gradient: bfloat16 [16384, 512], P(('ctx', 'head'))
Inputs may be any that keep to these rules, and one draw needn't show every extreme that they name: gate_block[b, h] is 0 for b = 0 and lies below b for every later block b.
All inputs are finite; a program needn't handle non-finite values.
Results may differ from a plain program's by a relative error of at most 0.0049.
Values may be sent and summed in bfloat16 or wider, within the bound.
A program may use at most 64 MiB of HBM per device.

v0:
```python
from functools import partial
import math

import jax
import jax.numpy as jnp
from jax import lax
from jax.sharding import PartitionSpec as P

KEY_BLOCK_TOKENS = 512


def score_terms(q_rows, o_rows, l_rows, d_rows, k_tile, v_tile, visible, score_scale):
    scores = (
        jnp.einsum("rhd,td->hrt", q_rows, k_tile, preferred_element_type=jnp.float32) * score_scale
    )
    weights = jnp.exp(scores - l_rows.T[:, :, None])
    if visible is not None:
        weights = jnp.where(visible[None], weights, 0.0)
    grad_weights = jnp.einsum("rhd,td->hrt", o_rows, v_tile, preferred_element_type=jnp.float32)
    grad_scores = weights * (grad_weights - d_rows.T[:, :, None])
    weights_low = weights.astype(jnp.bfloat16)
    slopes = grad_scores.astype(jnp.bfloat16)
    grad_q = (
        jnp.einsum("hrt,td->rhd", slopes, k_tile, preferred_element_type=jnp.float32) * score_scale
    )
    grad_k = (
        jnp.einsum("hrt,rhd->td", slopes, q_rows, preferred_element_type=jnp.float32) * score_scale
    )
    grad_v = jnp.einsum("hrt,rhd->td", weights_low, o_rows, preferred_element_type=jnp.float32)
    return (grad_q, jnp.concatenate([grad_k, grad_v], axis=1))


def add_slot(grad_slots, slot, offset, update):
    current = lax.dynamic_slice(
        grad_slots, (slot, offset, 0), (1, update.shape[0], update.shape[1])
    )
    return lax.dynamic_update_slice(grad_slots, current + update[None], (slot, offset, 0))


def keep_same(inner):
    return inner


def shards(queries, keys, values, out_grad, lse, delta, gate_block):
    ctx_index = lax.axis_index("ctx")
    group_index = lax.axis_index("head")
    q_local, o_local, k_local, v_local = (
        lax.all_to_all(queries, "head", split_axis=1, concat_axis=0, tiled=True),
        lax.all_to_all(out_grad, "head", split_axis=1, concat_axis=0, tiled=True),
        lax.all_to_all(keys, "head", split_axis=1, concat_axis=0, tiled=True),
        lax.all_to_all(values, "head", split_axis=1, concat_axis=0, tiled=True),
    )
    row_count, head_count = lse.shape
    head_dim = k_local.shape[1]
    score_scale = 1.0 / math.sqrt(head_dim)
    q_heads = q_local.reshape(row_count, head_count, head_dim)
    o_heads = o_local.reshape(row_count, head_count, head_dim)
    row_first = ctx_index * row_count
    row_last = row_first + row_count - 1
    own_block = row_first // KEY_BLOCK_TOKENS
    row_pos = row_first + jnp.arange(row_count, dtype=jnp.int32)
    gates = lax.dynamic_slice(gate_block, (own_block, group_index * head_count), (1, head_count))[0]
    slot_block = jnp.concatenate([own_block[None], jnp.where(gates != own_block, gates, -1)])

    def own_work(totals, k_tile, v_tile, key_start):
        grad_q, grad_slots = totals
        key_pos = key_start + jnp.arange(k_tile.shape[0], dtype=jnp.int32)
        visible = row_pos[:, None] >= key_pos[None, :]
        part_q, part_kv = score_terms(
            q_heads, o_heads, lse, delta, k_tile, v_tile, visible, score_scale
        )
        return (grad_q + part_q, add_slot(grad_slots, 0, key_start % KEY_BLOCK_TOKENS, part_kv))

    def gate_work(totals, head, k_tile, v_tile, key_start):
        grad_q, grad_slots = totals
        part_q, part_kv = score_terms(
            q_heads[:, head : head + 1],
            o_heads[:, head : head + 1],
            lse[:, head : head + 1],
            delta[:, head : head + 1],
            k_tile,
            v_tile,
            None,
            score_scale,
        )
        grad_q = grad_q.at[:, head : head + 1].add(part_q)
        return (grad_q, add_slot(grad_slots, head + 1, key_start % KEY_BLOCK_TOKENS, part_kv))

    zero_query = jnp.zeros((row_count, head_count, head_dim), jnp.float32)
    empty = (zero_query, jnp.zeros((head_count + 1, KEY_BLOCK_TOKENS, 2 * head_dim), jnp.float32))
    k_piece = lax.all_gather(k_local, "ctx", axis=0, tiled=True)
    v_piece = lax.all_gather(v_local, "ctx", axis=0, tiled=True)
    tile_size = math.gcd(k_piece.shape[0], KEY_BLOCK_TOKENS)

    def tile_step(step, inner_totals):
        tile_start = step * tile_size
        k_tile = lax.dynamic_slice_in_dim(k_piece, step * tile_size, tile_size, 0)
        v_tile = lax.dynamic_slice_in_dim(v_piece, step * tile_size, tile_size, 0)
        tile_block = tile_start // KEY_BLOCK_TOKENS
        inner_totals = lax.cond(
            (tile_block == own_block) & (tile_start <= row_last),
            partial(own_work, k_tile=k_tile, v_tile=v_tile, key_start=tile_start),
            keep_same,
            inner_totals,
        )
        for head in range(head_count):
            inner_totals = lax.cond(
                tile_block == slot_block[head + 1],
                partial(gate_work, head=head, k_tile=k_tile, v_tile=v_tile, key_start=tile_start),
                keep_same,
                inner_totals,
            )
        return inner_totals

    grad_q, grad_slots = lax.fori_loop(0, k_piece.shape[0] // tile_size, tile_step, empty)
    quarter = KEY_BLOCK_TOKENS // row_count
    slot_tiles = grad_slots.reshape(head_count + 1, quarter, row_count, 2 * head_dim)
    row_total = lax.axis_size("ctx") * row_count
    tiles = row_total // row_count
    tile_first = jnp.arange(tiles, dtype=jnp.int32)
    tile_block = tile_first // quarter
    tile_offset = tile_first % quarter
    picked = (tile_block[:, None, None] == slot_block[None, :, None]) & (
        tile_offset[:, None, None] == jnp.arange(quarter, dtype=jnp.int32)[None, None, :]
    )
    term = jnp.einsum(
        "tsq,sqrc->trc", picked.astype(jnp.float32), slot_tiles, precision=lax.Precision.HIGHEST
    )
    summed = lax.psum_scatter(
        term.reshape(row_total, 2 * head_dim), "ctx", scatter_dimension=0, tiled=True
    )
    query_low = grad_q.reshape(row_count, head_count * head_dim).astype(jnp.bfloat16)
    key_low = summed[:, :head_dim].astype(jnp.bfloat16)
    value_low = summed[:, head_dim:].astype(jnp.bfloat16)
    grad_queries, key_gradient, value_gradient = (
        lax.all_to_all(query_low, "head", split_axis=0, concat_axis=1, tiled=True),
        lax.all_to_all(key_low, "head", split_axis=0, concat_axis=1, tiled=True),
        lax.all_to_all(value_low, "head", split_axis=0, concat_axis=1, tiled=True),
    )
    return (grad_queries, key_gradient, value_gradient)


def solution(mesh):
    placed = (
        P(("ctx", "head"), None),
        P(("ctx", "head"), None),
        P(("ctx", "head"), None),
        P(("ctx", "head"), None),
        P("ctx", "head"),
        P("ctx", "head"),
        P(),
    )
    return jax.shard_map(
        shards,
        mesh=mesh,
        in_specs=placed,
        out_specs=(P(("ctx", "head"), None), P(("ctx", "head"), None), P(("ctx", "head"), None)),
        check_vma=False,
    )
```

profile of v0, /device:TPU:2, one launch (start us, length us, event | category | flops | bytes accessed | tf_op | source)
XLA Modules:
  0.0 994.4 jit_solution(9071908123988413301)
XLA Ops:
  8.0 7.6 all_to_all.124
  16.5 7.2 all_to_all.125
  23.7 1.9 copy.75
  25.6 5.3 all-to-all-start.2
  30.9 1.9 copy.74
  33.6 4.9 all-to-all-done.2
  38.6 5.1 all-to-all-start.3
  44.0 6.9 all-to-all-done.3
  51.0 94.6 %all-gather.3.cloned.1.call-done = bf16[16384,128]{1,0:T(8,128)(2,1)} async-done(((bf16[256,128]{1,0:T(8,128)(2,1)}), bf16[16384,128]{1,0:T(8,128)(2,1)}) %all-gather.3.cloned.1.call-update) | async-done | bytes 4194320 | tf_op jit(solution)/shard_map/all_gather | solution.py:91
  145.6 128.1 %all-gather.5.cloned.1.call-done = bf16[16384,128]{1,0:T(8,128)(2,1)} async-done(((bf16[256,128]{1,0:T(8,128)(2,1)}), bf16[16384,128]{1,0:T(8,128)(2,1)}) %all-gather.5.cloned.1.call-update) | async-done | bytes 4194320 | tf_op jit(solution)/shard_map/all_gather | solution.py:92
  273.8 2.7 broadcast_in_dim.70
  276.5 227.7 %while.26 = (s32[]{:T(128)}, f32[256,8,128]{2,0,1:T(8,128)S(1)}, f32[9,512,256]{1,2,0:T(8,128)}, s32[8]{0:T(128)S(1)}, s32[]{:T(128)}, /*index=5*/s32[]{:T(128)}...) while((s32[]{:T(128)}, f32[256,8,128]{2,0,1:T(8,128)S(1)}, ...), condition=%wide.region_19.20_spmd.clone, body=%wide.region_0.19_spmd.clone.sunk | while | flops 2705261312 | bytes 69549432 | solution.py:115
  282.1 1.0 constant_dynamic-slice_fusion.3
  283.1 7.0 conditional.27
  284.0 1.0 fusion.12
  285.0 1.4 fusion.3
  288.2 1.9 fusion.17
  295.8 1.0 constant_dynamic-slice_fusion.3
  302.7 1.0 constant_dynamic-slice_fusion.3
  309.6 1.0 constant_dynamic-slice_fusion.3
  316.5 1.0 constant_dynamic-slice_fusion.3
  323.4 1.0 constant_dynamic-slice_fusion.3
  330.3 1.0 constant_dynamic-slice_fusion.3
  337.2 1.0 constant_dynamic-slice_fusion.3
  344.1 1.0 constant_dynamic-slice_fusion.3
  351.1 1.0 constant_dynamic-slice_fusion.3
  358.0 1.0 constant_dynamic-slice_fusion.3
  364.9 1.0 constant_dynamic-slice_fusion.3
  371.8 1.0 constant_dynamic-slice_fusion.3
  378.7 1.0 constant_dynamic-slice_fusion.3
  385.6 1.0 constant_dynamic-slice_fusion.3
  392.5 1.0 constant_dynamic-slice_fusion.3
  399.4 1.0 constant_dynamic-slice_fusion.3
  427.0 1.0 constant_dynamic-slice_fusion.3
  433.9 1.0 constant_dynamic-slice_fusion.3
  496.1 1.0 constant_dynamic-slice_fusion.3
  503.0 1.0 constant_dynamic-slice_fusion.3
  504.2 6.8 reshape.722
  511.0 8.9 copy.49
  519.9 9.5 convolution_bitcast_fusion.9
  529.5 19.3 %copy.50 = f32[64,256,256]{2,1,0:T(8,128)} copy(f32[64,256,256]{2,0,1:T(8,128)S(1)} %convolution_bitcast_fusion.9) | data formatting | bytes 33554432 | tf_op jit(solution)/shard_map/tsq,sqrc->trc/dot_general | solution.py:126
  549.2 1.0 convert_element_type.179
  550.2 4.9 all-to-all-start.4
  555.1 416.7 %reduce-scatter.2.cloned.1.call-done = f32[256,256]{1,0:T(8,128)} async-done(((f32[16384,256]{1,0:T(8,128)}), f32[256,256]{1,0:T(8,128)}) %reduce-scatter.2.cloned.1.call-update) | async-done | bytes 262160 | tf_op jit(solution)/shard_map/reduce_scatter | solution.py:129
  973.5 4.1 all-to-all-start.5
  978.4 1.4 all-to-all-done.5
  979.9 5.1 all-to-all-start.6
  985.6 1.6 all-to-all-done.6
  (402 shorter events, 47.8 us)
Async XLA Ops:
  7.2 0.8 copy-start
  7.2 138.4 %all-gather.3.cloned.1.call-start = ((), (), s32[]{:S(2)}) async-start(), calls=%async_computation.8 | async-start | bytes 4259840 | tf_op jit(solution)/shard_map/all_gather | solution.py:91
  15.6 258.1 %all-gather.5.cloned.1.call-start = ((), (), s32[]{:S(2)}) async-start(), calls=%async_computation.9 | async-start | bytes 4259840 | tf_op jit(solution)/shard_map/all_gather | solution.py:92
  25.6 13.0 %all-to-all-start.2 = ((bf16[64,4,1024]{2,0,1:T(8,128)(2,1)}), bf16[64,4,1024]{2,0,1:T(8,128)(2,1)S(1)}, u32[]{:S(2)}, u32[]{:S(2)}) async-start(bf16[64,4,1024]{2,0,1:T(8,128)(2,1)} %bitcast.584), calls=%async_computation.2 | async-start | bytes 1048576 | tf_op jit(solution)/shard_map/all_to_all | solution.py:48
  38.6 12.3 %all-to-all-start.3 = ((bf16[64,4,1024]{2,0,1:T(8,128)(2,1)}), bf16[64,4,1024]{2,0,1:T(8,128)(2,1)S(1)}, u32[]{:S(2)}, u32[]{:S(2)}) async-start(bf16[64,4,1024]{2,0,1:T(8,128)(2,1)} %bitcast.583), calls=%async_computation.3 | async-start | bytes 1048576 | tf_op jit(solution)/shard_map/all_to_all | solution.py:49
  43.7 928.2 %reduce-scatter.2.cloned.1.call-start = ((), (), s32[]{:S(2)}) async-start(), calls=%async_computation.10 | async-start | bytes 17039360 | tf_op jit(solution)/shard_map/reduce_scatter | solution.py:129
  43.9 232.6 %copy-start.2 = (f32[256,8]{0,1:T(8,128)S(1)}, f32[256,8]{0,1:T(8,128)}, u32[]{:S(2)}) copy-start(f32[256,8]{0,1:T(8,128)} %param.47) | copy-start | bytes 24580
  43.9 232.6 %copy-start.3 = (f32[256,8]{0,1:T(8,128)S(1)}, f32[256,8]{0,1:T(8,128)}, u32[]{:S(2)}) copy-start(f32[256,8]{0,1:T(8,128)} %param.48) | copy-start | bytes 24580
  548.8 439.1 %copy-start.1 = (bf16[64,512]{1,0:T(8,128)(2,1)S(1)}, bf16[64,512]{1,0:T(8,128)(2,1)}, u32[]{:S(2)}) copy-start(bf16[64,512]{1,0:T(8,128)(2,1)} %param.44) | copy-start | bytes 196612
  550.2 423.2 %all-to-all-start.4 = ((bf16[4,64,1024]{2,1,0:T(8,128)(2,1)}), bf16[4,64,1024]{2,1,0:T(8,128)(2,1)S(1)}, u32[]{:S(2)}, u32[]{:S(2)}) async-start(bf16[4,64,1024]{2,1,0:T(8,128)(2,1)} %convert_element_type.179), calls=%async_computation.4 | async-start | bytes 1048576 | tf_op jit(solution)/shard_map/all_to_all | solution.py:136
  973.5 6.4 all-to-all-start.5
  979.9 7.4 all-to-all-start.6
Sparse Core Ops, SparseCore 0:
  15.7 129.7 all-gather.2
  149.1 124.5 all-gather.4
  548.9 422.9 reduce-scatter.1
where the time goes:
time: 1000 us; the launch traced here: 994 us
  waiting for transfers between devices  654 us (65%)
  loops' own time  167 us (17%)
  local copies, waits for them, and re-layouts  101 us (10%)
  starting transfers between devices  24.6 us (2%)
  blocking collectives  14.7 us (1%)
  matrix products  14.4 us (1%)
  between operations  13.9 us (1%)
    reduce_scatter x1, waiting for transfers between devices, shards(): lax.psum_scatter(term.reshape(row_total, 2 * head_dim), 'ctx', scatter_di...  417 us
    another operation x1, loops' own time, shards(): lax.fori_loop(0, k_piece.shape[0] // tile_size, tile_step, empty)  162 us
    all_gather x1, waiting for transfers between devices, shards(): v_piece = lax.all_gather(v_local, 'ctx', axis=0, tiled=True)  128 us
    all_gather x1, waiting for transfers between devices, shards(): k_piece = lax.all_gather(k_local, 'ctx', axis=0, tiled=True)  94.6 us
    dynamic_slice x32, local copies, waits for them, and re-layouts, tile_step(): v_tile = lax.dynamic_slice_in_dim(v_piece, step * tile_size, tile_size, 0)  31.8 us
    slice x32, local copies, waits for them, and re-layouts, tile_step(): slot_block[head + 1]  21.9 us
  transfers between devices with their start and end apart: 8, of which 7 were waited for; matrix products, arithmetic and copies ran while one was open for 1% of the time, Pallas kernels for 0%

commit v1 on v0

v1 whole, which is shorter than its diff:
```python
import math

import jax
import jax.numpy as jnp
from jax import lax
from jax.experimental import pallas as pl
from jax.experimental.pallas import tpu as pltpu
from jax.sharding import PartitionSpec as P

MESH = pl.DeviceIdType.MESH
LOG2E = math.log2(math.e)
SCALE = 1.0 / math.sqrt(128.0)
F32 = jnp.float32
BF16 = jnp.bfloat16


def flip(bit, by):
    return bit if by == 0 else 1 - bit


def xor(a, b):
    return lax.rem(a + b, 2)


class Place:
    def __init__(self):
        ctx, head = lax.axis_index("ctx"), lax.axis_index("head")
        self.z = ctx // 8
        self.X = lax.rem(ctx // 4, 2)
        self.Y = lax.rem(ctx // 2, 2)
        self.yl = lax.rem(ctx, 2)
        self.xl = head // 2
        self.c = lax.rem(head, 2)
        self.gx, self.gy = xor(self.xl, self.X), xor(self.yl, self.Y)
        self.g = self.gx * 2 + self.gy
        self.e = self.g * 2 + self.c
        self.s = self.yl * 4 + self.xl * 2 + self.c
        self.m = self.X * 4 + self.Y * 2 + self.c
        self.b = self.z * 4 + self.X * 2 + self.Y

    def inner(self, k):
        yl, xl, c = flip(self.yl, k // 4), flip(self.xl, k // 2 % 2), flip(self.c, k % 2)
        e = (xor(xl, self.X) * 2 + xor(yl, self.Y)) * 2 + c
        return device(self.z, self.X, xl, self.Y, yl, c), yl * 4 + xl * 2 + c, e

    def row(self, k):
        X, Y, c = flip(self.X, k // 4), flip(self.Y, k // 2 % 2), flip(self.c, k % 2)
        return device(self.z, X, xor(self.gx, X), Y, xor(self.gy, Y), c), X * 4 + Y * 2 + c

    def above(self):
        return {"ctx": lax.rem(self.z + 1, 8) * 8 + self.X * 4 + self.Y * 2 + self.yl}

    def below(self):
        return {"ctx": lax.rem(self.z + 7, 8) * 8 + self.X * 4 + self.Y * 2 + self.yl}

    def barrier_signal(self, sem):
        for k in range(1, 32):
            to = device(
                self.z,
                flip(self.X, k // 16),
                flip(self.xl, k // 8 % 2),
                flip(self.Y, k // 4 % 2),
                flip(self.yl, k // 2 % 2),
                flip(self.c, k % 2),
            )
            pl.semaphore_signal(sem, inc=1, device_id=to, device_id_type=MESH)
        for to in (self.above(), self.below()):
            pl.semaphore_signal(sem, inc=1, device_id=to, device_id_type=MESH)


BARRIER_COUNT = 33


def device(z, X, xl, Y, yl, c):
    return {"ctx": z * 8 + X * 4 + Y * 2 + yl, "head": xl * 2 + c}


def remote(src, dst, send, recv, to):
    return pltpu.make_async_remote_copy(
        src_ref=src, dst_ref=dst, send_sem=send, recv_sem=recv, device_id=to, device_id_type=MESH
    )


def ring_steps():
    return [(t, h) for t in range(3) for h in range(2)]


def gather_kernel(
    tab,
    q_ref,
    o_ref,
    k_ref,
    v_ref,
    ld_ref,
    q_in,
    o_in,
    own_kv,
    gkv,
    ld_in,
    kvl,
    kvz,
    picked,
    q_send,
    q_recv,
    ld_send,
    ld_recv,
    p_send,
    p_recv,
    z_send,
    z_recv,
    r_send,
    r_recv,
    l_sem,
):
    me = Place()
    barrier = pltpu.get_barrier_semaphore()
    me.barrier_signal(barrier)
    for g in range(4):
        kvl[g, :, :128] = k_ref[:, g * 128 : (g + 1) * 128]
        kvl[g, :, 128:] = v_ref[:, g * 128 : (g + 1) * 128]
    pl.semaphore_wait(barrier, BARRIER_COUNT)

    staying = (me.xl == me.X) & (me.yl == me.Y)
    sends = []
    for g in range(4):
        X, Y = me.xl, me.yl
        to = device(me.z, X, xor(X, g // 2), Y, xor(Y, g % 2), me.c)
        copy = remote(kvl.at[g], kvz.at[me.b], p_send.at[g], p_recv.at[me.X * 2 + me.Y], to)
        if g == 0:

            @pl.when(staying)
            def _():
                kvz[me.b] = kvl[0]

            @pl.when(jnp.logical_not(staying))
            def _():
                copy.start()
        else:
            copy.start()
        sends.append(copy)

    mine = []
    for k in range(1, 8):
        to, _, e = me.inner(k)
        mine.append(remote(kvl.at[e // 2], own_kv.at[me.s], q_send.at[2, k], q_recv.at[2, k], to))
        mine[-1].start()
    for k in range(1, 8):
        to, _, e = me.inner(k)
        cols = pl.ds(pl.multiple_of(e * 512, 512), 512)
        for i, (src, dst) in enumerate(((q_ref, q_in), (o_ref, o_in))):
            mine.append(
                remote(src.at[:, cols], dst.at[me.s], q_send.at[i, k], q_recv.at[i, k], to)
            )
            mine[-1].start()
    cols = pl.ds(pl.multiple_of(me.e * 512, 512), 512)
    local = [
        pltpu.make_async_copy(src.at[:, cols], dst.at[me.s], l_sem.at[i])
        for i, (src, dst) in enumerate(((q_ref, q_in), (o_ref, o_in)))
    ]
    for copy in local:
        copy.start()
    own_kv[me.s] = kvl[me.g]

    ld_yl = xor(me.c, me.Y)
    ld_xl = xor(me.xl, me.X)
    ld_copies = []
    for core in range(2):
        to = device(me.z, me.X, ld_xl, me.Y, ld_yl, core)
        here = (ld_xl == me.xl) & (ld_yl == me.yl) & (me.c == core)
        copy = remote(ld_ref, ld_in.at[me.yl], ld_send.at[core], ld_recv.at[me.yl], to)

        @pl.when(here)
        def _():
            ld_in[me.yl] = ld_ref[...]

        @pl.when(jnp.logical_not(here))
        def _():
            copy.start()

        ld_copies.append((here, copy))

    def chunk(d, half):
        return kvz.at[pl.ds(lax.rem(d + 8, 8) * 4 + half * 2, 2)]

    ring = []

    def pass_on(way, t, half):
        d = me.z - t if way == 0 else me.z + t
        part = chunk(d, half)
        copy = remote(
            part,
            part,
            z_send.at[way, t, half],
            z_recv.at[way, t, half],
            me.above() if way == 0 else me.below(),
        )
        copy.start()
        ring.append(copy)

    def arrived(way, t, half):
        d = me.z - t - 1 if way == 0 else me.z + t + 1
        part = chunk(d, half)
        remote(
            part, part, z_send.at[way, t, half], z_recv.at[way, t, half], me.above()
        ).wait_recv()

    for half in range(2):
        for Y in range(2):
            w = half * 2 + Y
            here = staying & (me.X * 2 + me.Y == w)
            block = kvz.at[me.z * 4 + w]

            @pl.when(jnp.logical_not(here))
            def _():
                remote(block, block, p_send.at[0], p_recv.at[w], me.above()).wait_recv()

        for way in range(2):
            pass_on(way, 0, half)
    for t in range(1, 4):
        for half in range(2):
            for way in range(2):
                arrived(way, t - 1, half)
                if t < 3 or half == way:
                    pass_on(way, t, half)
    for way in range(2):
        arrived(way, 3, way)

    rows = []
    for k in (7, 6, 5, 4, 3, 2, 1, 0):
        to, p = me.row(k)
        for h in range(4):
            got = kvz[tab[0, p * 4 + h]]
            if k == 0:
                gkv[me.m, h] = got
            else:
                picked[k, h] = got
        if k:
            copy = remote(picked.at[k], gkv.at[me.m], r_send.at[k], r_recv.at[k], to)
            copy.start()
            rows.append(copy)

    for copy in local:
        copy.wait()
    for copy in mine:
        copy.wait_send()
    for k in range(1, 8):
        _, s, _ = me.inner(k)
        for i, dst in enumerate((q_in, o_in, own_kv)):
            part = dst.at[s]
            remote(part, part, q_send.at[i, k], q_recv.at[i, k], me.above()).wait_recv()
    for here, copy in ld_copies:

        @pl.when(jnp.logical_not(here))
        def _():
            copy.wait_send()

    for yl in range(2):
        here = (me.gx == me.xl) & (me.gy == me.c) & (me.yl == yl)
        part = ld_in.at[yl]

        @pl.when(jnp.logical_not(here))
        def _():
            remote(part, part, ld_send.at[0], ld_recv.at[yl], me.above()).wait_recv()

    @pl.when(jnp.logical_not(staying))
    def _():
        sends[0].wait_send()

    for copy in sends[1:] + ring + rows:
        copy.wait_send()
    for k in range(1, 8):
        _, p = me.row(k)
        part = gkv.at[p]
        remote(part, part, r_send.at[k], r_recv.at[k], me.above()).wait_recv()


def dot(a, b, contract):
    return lax.dot_general(a, b, ((contract[:1], contract[1:]), ((), ())), preferred_element_type=F32)


def terms(q, o, lse, delta, k, v, mask):
    scores = dot(k, q, (1, 1)) * (SCALE * LOG2E)
    weights = jnp.exp2(scores - lse)
    if mask is not None:
        weights = jnp.where(mask, weights, 0.0)
    slopes = weights * (dot(v, o, (1, 1)) - delta)
    return weights.astype(BF16), slopes.astype(BF16)


def attend_kernel(tab, q_in, o_in, own_kv, gkv, ld_in, dq_out, own_out, gate_out):
    me = Place()
    tile = 256
    key_pos = lax.broadcasted_iota(jnp.int32, (tile, tile), 0)
    query_pos = lax.broadcasted_iota(jnp.int32, (tile, tile), 1)
    causal = key_pos <= query_pos
    own = own_kv[...].reshape(512, 256)
    own_k, own_v = own[:, :128], own[:, 128:]
    own_dk = [jnp.zeros((tile, 128), F32) for _ in range(2)]
    own_dv = [jnp.zeros((tile, 128), F32) for _ in range(2)]
    for h in range(4):
        lanes = slice(h * 128, (h + 1) * 128)
        q = q_in[:, :, lanes].reshape(512, 128)
        o = o_in[:, :, lanes].reshape(512, 128)
        row = 4 * me.c + h
        lse = jnp.concatenate([ld_in[i, pl.ds(row, 1), :] for i in range(2)], axis=1) * LOG2E
        delta = jnp.concatenate([ld_in[i, pl.ds(row + 8, 1), :] for i in range(2)], axis=1)
        gate_on = tab[0, me.m * 4 + h] != me.b
        gate_lse = jnp.where(gate_on, lse, 1e30)
        gk = gkv[:, h, :, :128].reshape(512, 128)
        gv = gkv[:, h, :, 128:].reshape(512, 128)
        gdk = [jnp.zeros((tile, 128), F32) for _ in range(2)]
        gdv = [jnp.zeros((tile, 128), F32) for _ in range(2)]
        for i in range(2):
            cols = slice(i * tile, (i + 1) * tile)
            qi, oi, di = q[cols], o[cols], delta[:, cols]
            dq = jnp.zeros((tile, 128), F32)
            for j in range(2):
                keys = slice(j * tile, (j + 1) * tile)
                w, s = terms(qi, oi, gate_lse[:, cols], di, gk[keys], gv[keys], None)
                gdv[j] += dot(w, oi, (1, 0))
                gdk[j] += dot(s, qi, (1, 0))
                dq += dot(s, gk[keys], (0, 0))
            for j in range(i + 1):
                keys = slice(j * tile, (j + 1) * tile)
                mask = causal if i == j else None
                w, s = terms(qi, oi, lse[:, cols], di, own_k[keys], own_v[keys], mask)
                own_dv[j] += dot(w, oi, (1, 0))
                own_dk[j] += dot(s, qi, (1, 0))
                dq += dot(s, own_k[keys], (0, 0))
            dq_out[i * 4 : (i + 1) * 4, :, lanes] = (dq * SCALE).astype(BF16).reshape(4, 64, 128)
        for j in range(2):
            part = jnp.concatenate([gdk[j] * SCALE, gdv[j]], axis=1).astype(BF16)
            gate_out[j * 4 : (j + 1) * 4, h] = part.reshape(4, 64, 256)
    for j in range(2):
        part = jnp.concatenate([own_dk[j] * SCALE, own_dv[j]], axis=1).astype(BF16)
        own_out[j * 4 : (j + 1) * 4] = part.reshape(4, 64, 256)


def scatter_kernel(
    tab,
    dq_ref,
    own_ref,
    gate_ref,
    out_q,
    out_k,
    out_v,
    own_in,
    gate_in,
    run,
    z_out,
    z_in,
    sum_out,
    sum_in,
    q_send,
    q_recv,
    r_send,
    r_recv,
    z_send,
    z_recv,
    p_send,
    p_recv,
    l_sem,
):
    me = Place()
    barrier = pltpu.get_barrier_semaphore()
    me.barrier_signal(barrier)
    gate_in[me.m] = gate_ref[me.m]
    own_in[me.e] = own_ref[me.s]
    run[32] = jnp.zeros((64, 256), F32)
    pl.semaphore_wait(barrier, BARRIER_COUNT)

    copies = []
    for k in (7, 6, 5, 4, 3, 2, 1):
        to, p = me.row(k)
        copies.append(remote(gate_ref.at[p], gate_in.at[me.m], r_send.at[k], r_recv.at[k], to))
        copies[-1].start()
    cols = pl.ds(pl.multiple_of(me.e * 512, 512), 512)
    for k in range(1, 8):
        to, s, _ = me.inner(k)
        copies.append(remote(dq_ref.at[s], out_q.at[:, cols], q_send.at[0, k], q_recv.at[0, k], to))
        copies[-1].start()
        copies.append(remote(own_ref.at[s], own_in.at[me.e], q_send.at[1, k], q_recv.at[1, k], to))
        copies[-1].start()
    local = pltpu.make_async_copy(dq_ref.at[me.s], out_q.at[:, cols], l_sem)
    local.start()

    for k in range(1, 8):
        _, p = me.row(k)
        part = gate_in.at[p]
        remote(part, part, r_send.at[k], r_recv.at[k], me.above()).wait_recv()

    def add(i, carry):
        run[i] = gate_in[i // 4, lax.rem(i, 4)].astype(F32) + run[tab[1, i]]
        return carry

    lax.fori_loop(0, 32, add, 0)

    def total(d, w):
        return run[tab[2, lax.rem(d + 8, 8) * 4 + w]]

    for t in range(4):
        for half in range(2):
            for way in range(2):
                if t == 0 and half != way:
                    continue
                d = me.z + 4 - t if way == 0 else me.z - 4 + t
                to = me.above() if way == 0 else me.below()
                if t >= 2 or (t == 1 and half == way):
                    part = z_in.at[way, t - 1, half]
                    remote(
                        part, part, z_send.at[way, t - 1, half], z_recv.at[way, t - 1, half], to
                    ).wait_recv()
                for i in range(2):
                    value = total(d, half * 2 + i)
                    if t >= 2 or (t == 1 and half == way):
                        value += z_in[way, t - 1, half, i].astype(F32)
                    z_out[way, t, half, i] = value.astype(BF16)
                copy = remote(
                    z_out.at[way, t, half],
                    z_in.at[way, t, half],
                    z_send.at[way, t, half],
                    z_recv.at[way, t, half],
                    to,
                )
                copy.start()
                copies.append(copy)
    staying = (me.xl == me.X) & (me.yl == me.Y)
    ends = []
    for half in range(2):
        for way in range(2):
            part = z_in.at[way, 3, half]
            remote(
                part, part, z_send.at[way, 3, half], z_recv.at[way, 3, half], me.above()
            ).wait_recv()
        for i in range(2):
            w = half * 2 + i
            value = total(me.z, w)
            for way in range(2):
                value += z_in[way, 3, half, i].astype(F32)
            sum_out[w] = value.astype(BF16)
            here = staying & (me.X * 2 + me.Y == w)
            to = device(me.z, w // 2, me.X, w % 2, me.Y, me.c)
            copy = remote(sum_out.at[w], sum_in.at[me.g], p_send.at[w], p_recv.at[me.g], to)

            @pl.when(here)
            def _():
                sum_in[0] = sum_out[w]

            @pl.when(jnp.logical_not(here))
            def _():
                copy.start()

            ends.append((here, copy))

    for k in range(1, 8):
        _, s, e = me.inner(k)
        part = own_in.at[e]
        remote(part, part, q_send.at[1, k], q_recv.at[1, k], me.above()).wait_recv()
    for g in range(4):
        part = sum_in.at[g]
        copy = remote(part, part, p_send.at[g], p_recv.at[g], me.above())
        if g == 0:

            @pl.when(jnp.logical_not(staying))
            def _():
                copy.wait_recv()
        else:
            copy.wait_recv()
        value = sum_in[g].astype(F32) + own_in[2 * g].astype(F32) + own_in[2 * g + 1].astype(F32)
        out_k[:, g * 128 : (g + 1) * 128] = value[:, :128].astype(BF16)
        out_v[:, g * 128 : (g + 1) * 128] = value[:, 128:].astype(BF16)

    local.wait()
    for k in range(1, 8):
        _, s, e = me.inner(k)
        part = out_q.at[:, pl.ds(pl.multiple_of(e * 512, 512), 512)]
        remote(part, part, q_send.at[0, k], q_recv.at[0, k], me.above()).wait_recv()
    for here, copy in ends:

        @pl.when(jnp.logical_not(here))
        def _():
            copy.wait_send()

    for copy in copies:
        copy.wait_send()


def vmem(count):
    return [pl.BlockSpec(memory_space=pltpu.VMEM)] * count


SMEM_SPEC = pl.BlockSpec(memory_space=pltpu.SMEM)
ANY_SPEC = pl.BlockSpec(memory_space=pl.ANY)
DMA = pltpu.SemaphoreType.DMA
VMEM_LIMIT = 48 * 1024 * 1024


def shape(*dims, dtype=BF16):
    return jax.ShapeDtypeStruct(dims, dtype)


def shards(queries, keys, values, out_grad, lse, delta, gate_block):
    ctx, head = lax.axis_index("ctx"), lax.axis_index("head")
    z, X, Y, yl, xl = ctx // 8, ctx // 4 % 2, ctx // 2 % 2, ctx % 2, head // 2
    g = (xl + X) % 2 * 2 + (yl + Y) % 2
    gates = lax.dynamic_slice(gate_block, (z * 4, g * 8), (4, 8)).reshape(32)
    slots = jnp.arange(32, dtype=jnp.int32)
    same = (gates[:, None] == gates[None, :]) & (slots[None, :] < slots[:, None])
    previous = jnp.max(jnp.where(same, slots[None, :], -1), axis=1)
    member = gates[None, :] == slots[:, None]
    last = jnp.max(jnp.where(member, slots[None, :], -1), axis=1)
    tab = jnp.stack([gates, jnp.where(previous < 0, 32, previous), jnp.where(last < 0, 32, last)])
    ld = jnp.concatenate([lse.T, delta.T], axis=0)

    q_in, o_in, own_kv, gkv, ld_in = pl.pallas_call(
        gather_kernel,
        out_shape=(
            shape(8, 64, 512),
            shape(8, 64, 512),
            shape(8, 64, 256),
            shape(8, 4, 64, 256),
            shape(2, 16, 256, dtype=F32),
        ),
        in_specs=[SMEM_SPEC] + vmem(5),
        out_specs=tuple(vmem(5)),
        scratch_shapes=[
            pltpu.VMEM((4, 64, 256), BF16),
            pltpu.VMEM((32, 64, 256), BF16),
            pltpu.VMEM((8, 4, 64, 256), BF16),
            DMA((3, 8)),
            DMA((3, 8)),
            DMA((2,)),
            DMA((2,)),
            DMA((4,)),
            DMA((4,)),
            DMA((2, 4, 2)),
            DMA((2, 4, 2)),
            DMA((8,)),
            DMA((8,)),
            DMA((2,)),
        ],
        compiler_params=pltpu.CompilerParams(
            collective_id=0, has_side_effects=True, vmem_limit_bytes=VMEM_LIMIT
        ),
        name="gather",
    )(tab, queries, out_grad, keys, values, ld)

    dq, own_part, gate_part = pl.pallas_call(
        attend_kernel,
        out_shape=(shape(8, 64, 512), shape(8, 64, 256), shape(8, 4, 64, 256)),
        in_specs=[SMEM_SPEC] + vmem(5),
        out_specs=tuple(vmem(3)),
        compiler_params=pltpu.CompilerParams(vmem_limit_bytes=VMEM_LIMIT),
        name="attend",
    )(tab, q_in, o_in, own_kv, gkv, ld_in)

    return pl.pallas_call(
        scatter_kernel,
        out_shape=(shape(64, 4096), shape(64, 512), shape(64, 512)),
        in_specs=[SMEM_SPEC] + vmem(3),
        out_specs=tuple(vmem(3)),
        scratch_shapes=[
            pltpu.VMEM((8, 64, 256), BF16),
            pltpu.VMEM((8, 4, 64, 256), BF16),
            pltpu.VMEM((33, 64, 256), F32),
            pltpu.VMEM((2, 4, 2, 2, 64, 256), BF16),
            pltpu.VMEM((2, 4, 2, 2, 64, 256), BF16),
            pltpu.VMEM((4, 64, 256), BF16),
            pltpu.VMEM((4, 64, 256), BF16),
            DMA((2, 8)),
            DMA((2, 8)),
            DMA((8,)),
            DMA((8,)),
            DMA((2, 4, 2)),
            DMA((2, 4, 2)),
            DMA((4,)),
            DMA((4,)),
            DMA(()),
        ],
        compiler_params=pltpu.CompilerParams(
            collective_id=1, has_side_effects=True, vmem_limit_bytes=VMEM_LIMIT
        ),
        name="scatter",
    )(tab, dq, own_part, gate_part)


def solution(mesh):
    rows = P(("ctx", "head"), None)
    return jax.shard_map(
        shards,
        mesh=mesh,
        in_specs=(rows, rows, rows, rows, P("ctx", "head"), P("ctx", "head"), P()),
        out_specs=(rows, rows, rows),
        check_vma=False,
    )
```

time: 1000 us -> 95.7 us (0.10)
  waiting for transfers between devices: 654 us -> 0 us
  loops' own time: 167 us -> 0 us
  local copies, waits for them, and re-layouts: 101 us -> 5.08 us
  Pallas kernels: 0 us -> 88.7 us
  starting transfers between devices: 24.6 us -> 0 us
  blocking collectives: 14.7 us -> 0 us
  matrix products: 14.4 us -> 0 us
  between operations: 13.9 us -> 0.87 us
    reduce_scatter x1 -> x0, waiting for transfers between devices: 417 us -> none  [shards(): lax.psum_scatter(term.reshape(row_total, 2 * head_dim), 'ctx', scatter_di...]
    all_gather x2 -> x0, waiting for transfers between devices: 223 us -> none  [the longest x1 128 us: shards(): v_piece = lax.all_gather(v_local, 'ctx', axis=0, tiled=True)]
    another operation x289 -> x0, loops' own time: 167 us -> none  [the longest x1 162 us: shards(): lax.fori_loop(0, k_piece.shape[0] // tile_size, tile_step, empty)]
    pallas_call x0 -> x3, Pallas kernels: none -> 88.7 us  [the longest x1 41.4 us: shards(): pl.pallas_call(gather_kernel, out_shape=(shape(8, 64, 512), shape(8, 64,...]
    dynamic_slice x32 -> x1, local copies, waits for them, and re-layouts: 31.8 us -> 0.77 us  [shards(): gates = lax.dynamic_slice(gate_block, (z * 4, g * 8), (4, 8)).reshape(32)]
    all_to_all x5 -> x0, starting transfers between devices: 24.5 us -> none  [the longest x1 5.3 us: shards(): lax.all_to_all(queries, 'head', split_axis=1, concat_axis=0, tiled=True)]
    slice x33 -> x0, local copies, waits for them, and re-layouts: 22.6 us -> none  [the longest x32 21.9 us: tile_step(): slot_block[head + 1]]
    dot_general x1 -> x0, local copies, waits for them, and re-layouts: 19.3 us -> none  [shards(): jnp.einsum('tsq,sqrc->trc', picked.astype(jnp.float32), slot_tiles, preci...]
  transfers between devices with their start and end apart: 8 -> 0, of which waited for: 7 -> 0; matrix products, arithmetic and copies ran while one was open for 1% -> 0% of each run, Pallas kernels for 0% -> 0%
where the time goes in v1:
time: 95.7 us; the launch traced here: 94.8 us
  Pallas kernels  88.7 us (93%)
  local copies, waits for them, and re-layouts  5.08 us (5%)
    pallas_call x1, Pallas kernels, shards(): pl.pallas_call(gather_kernel, out_shape=(shape(8, 64, 512), shape(8, 64,...  41.4 us
    pallas_call x1, Pallas kernels, shards(): pl.pallas_call(scatter_kernel, out_shape=(shape(64, 4096), shape(64, 512)...  39.2 us
    pallas_call x1, Pallas kernels, shards(): pl.pallas_call(attend_kernel, out_shape=(shape(8, 64, 512), shape(8, 64,...  8.11 us
    unnamed x15, local copies, waits for them, and re-layouts  4.15 us

profile of v1, /device:TPU:2, one launch (start us, length us, event | category | flops | bytes accessed | tf_op | source)
XLA Modules:
  0.0 94.8 jit_solution(9669702523605433950)
XLA Ops:
  0.7 0.0 copy-start.5
  0.7 0.0 copy-start.4
  0.7 0.0 copy-start.2
  0.7 0.0 copy-start.3
  0.8 0.8 dynamic_slice.3
  1.6 0.1 eq.30
  1.6 0.1 stack_reshape.3
  1.7 0.2 select_reduce_fusion.1
  1.9 0.0 copy-done.5
  1.9 0.0 copy-done.4
  2.0 0.0 copy-done.2
  2.0 0.0 copy-done.3
  2.0 0.0 copy-start
  2.0 1.0 %copy-done = bf16[64,4096]{1,0:T(8,128)(2,1)S(1)} copy-done((bf16[64,4096]{1,0:T(8,128)(2,1)S(1)}, bf16[64,4096]{1,0:T(8,128)(2,1)}, u32[]{:S(2)}) %copy-start) | copy-done | bytes 524312
  3.0 0.0 copy-start.1
  3.0 1.0 %copy-done.1 = bf16[64,4096]{1,0:T(8,128)(2,1)S(1)} copy-done((bf16[64,4096]{1,0:T(8,128)(2,1)S(1)}, bf16[64,4096]{1,0:T(8,128)(2,1)}, u32[]{:S(2)}) %copy-start.1) | copy-done | bytes 524312
  4.1 41.4 %gather.1 = (bf16[8,64,512]{2,1,0:T(8,128)(2,1)S(1)}, bf16[8,64,512]{2,1,0:T(8,128)(2,1)S(1)}, bf16[8,64,256]{2,1,0:T(8,128)(2,1)S(1)}, bf16[8,4,64,256]{3,2,1,0:T(8,128)(2,1)S(1)}, f32[2,16,256]{2,1,0:T(8,128)S(1)}) custom-call(s32[3,32]{1,0:T(4,128)S(1)} %pad_add_fusion.tab, bf16[64,4096]{1,0:T(8,128)(2,1)S(1)} %copy-done, bf16[64,4096]{1,0:T(8,128)(2,1)S(1)} %copy-done.1, ...), custom_call_target="tpu_custom_call" | custom-call | tf_op jit(solution)/shard_map/gather/pallas_call | solution.py:515
  45.5 8.1 %attend.1 = (bf16[8,64,512]{2,1,0:T(8,128)(2,1)S(1)}, bf16[8,64,256]{2,1,0:T(8,128)(2,1)S(1)}, bf16[8,4,64,256]{3,2,1,0:T(8,128)(2,1)S(1)}) custom-call(s32[3,32]{1,0:T(4,128)S(1)} %pad_add_fusion.tab, bf16[8,64,512]{2,1,0:T(8,128)(2,1)S(1)} %get-tuple-element.11.q_in, bf16[8,64,512]{2,1,0:T(8,128)(2,1)S(1)} %get-tuple-element.12.o_in, ...), custom_call_target="tpu_custom_call" | custom-call | tf_op jit(solution)/shard_map/attend/pallas_call | solution.py:548
  53.6 39.2 %scatter.1 = (bf16[64,4096]{1,0:T(8,128)(2,1)S(1)}, bf16[64,512]{1,0:T(8,128)(2,1)S(1)}, bf16[64,512]{1,0:T(8,128)(2,1)S(1)}) custom-call(s32[3,32]{1,0:T(4,128)S(1)} %pad_add_fusion.tab, bf16[8,64,512]{2,1,0:T(8,128)(2,1)S(1)} %get-tuple-element.16.dq_ref, bf16[8,64,256]{2,1,0:T(8,128)(2,1)S(1)} %get-tuple-element.17.own_ref, ...), custom_call_target="tpu_custom_call" | custom-call | tf_op jit(solution)/shard_map/scatter/pallas_call | solution.py:557
  92.8 0.8 copy.13
  93.5 0.6 copy.14
  94.2 0.6 copy.15
  (3 shorter events, 0.0 us)
Async XLA Ops:
  0.7 1.2 %copy-start.5 = (f32[256,8]{0,1:T(8,128)S(1)}, f32[256,8]{0,1:T(8,128)}, u32[]{:S(2)}) copy-start(f32[256,8]{0,1:T(8,128)} %param.11) | copy-start | bytes 24580
  0.7 1.2 %copy-start.4 = (f32[256,8]{0,1:T(8,128)S(1)}, f32[256,8]{0,1:T(8,128)}, u32[]{:S(2)}) copy-start(f32[256,8]{0,1:T(8,128)} %param.12) | copy-start | bytes 24580
  0.7 1.2 %copy-start.2 = (bf16[64,512]{1,0:T(8,128)(2,1)S(1)}, bf16[64,512]{1,0:T(8,128)(2,1)}, u32[]{:S(2)}) copy-start(bf16[64,512]{1,0:T(8,128)(2,1)} %k_ref.1) | copy-start | bytes 196612
  0.7 1.2 %copy-start.3 = (bf16[64,512]{1,0:T(8,128)(2,1)S(1)}, bf16[64,512]{1,0:T(8,128)(2,1)}, u32[]{:S(2)}) copy-start(bf16[64,512]{1,0:T(8,128)(2,1)} %v_ref.1) | copy-start | bytes 196612
  2.0 1.0 %copy-start = (bf16[64,4096]{1,0:T(8,128)(2,1)S(1)}, bf16[64,4096]{1,0:T(8,128)(2,1)}, u32[]{:S(2)}) copy-start(bf16[64,4096]{1,0:T(8,128)(2,1)} %q_ref.1) | copy-start | bytes 1572868
  3.0 1.0 %copy-start.1 = (bf16[64,4096]{1,0:T(8,128)(2,1)S(1)}, bf16[64,4096]{1,0:T(8,128)(2,1)}, u32[]{:S(2)}) copy-start(bf16[64,4096]{1,0:T(8,128)(2,1)} %o_ref.1) | copy-start | bytes 1572868

commit v2 on v0

v2 whole, which is shorter than its diff:
```python
import math

import jax
import jax.numpy as jnp
from jax import lax
from jax.experimental import pallas as pl
from jax.experimental.pallas import tpu as pltpu
from jax.sharding import PartitionSpec as P

MESH = pl.DeviceIdType.MESH
LOG2E = math.log2(math.e)
SCALE = 1.0 / math.sqrt(128.0)
F32 = jnp.float32
BF16 = jnp.bfloat16
PARTS = 2
PART = 64 // PARTS


def flip(bit, by):
    return bit if by == 0 else 1 - bit


def xor(a, b):
    return lax.rem(a + b, 2)


class Place:
    def __init__(self):
        ctx, head = lax.axis_index("ctx"), lax.axis_index("head")
        self.z = ctx // 8
        self.X = lax.rem(ctx // 4, 2)
        self.Y = lax.rem(ctx // 2, 2)
        self.yl = lax.rem(ctx, 2)
        self.xl = head // 2
        self.c = lax.rem(head, 2)
        self.gx, self.gy = xor(self.xl, self.X), xor(self.yl, self.Y)
        self.g = self.gx * 2 + self.gy
        self.e = self.g * 2 + self.c
        self.s = self.yl * 4 + self.xl * 2 + self.c
        self.m = self.X * 4 + self.Y * 2 + self.c
        self.b = self.z * 4 + self.X * 2 + self.Y

    def inner(self, k):
        yl, xl, c = flip(self.yl, k // 4), flip(self.xl, k // 2 % 2), flip(self.c, k % 2)
        e = (xor(xl, self.X) * 2 + xor(yl, self.Y)) * 2 + c
        return device(self.z, self.X, xl, self.Y, yl, c), yl * 4 + xl * 2 + c, e

    def row(self, k):
        X, Y, c = flip(self.X, k // 4), flip(self.Y, k // 2 % 2), flip(self.c, k % 2)
        return device(self.z, X, xor(self.gx, X), Y, xor(self.gy, Y), c), X * 4 + Y * 2 + c

    def plane(self, step):
        return lax.rem(self.z + step, 8)

    def taker(self, d, g):
        return device(d, self.xl, xor(self.xl, g // 2), self.yl, xor(self.yl, g % 2), self.c)

    def owner(self, d, w):
        return device(d, w // 2, self.X, w % 2, self.Y, self.c)

    def above(self):
        return {"ctx": lax.rem(self.z + 1, 8) * 8 + self.X * 4 + self.Y * 2 + self.yl}

    def below(self):
        return {"ctx": lax.rem(self.z + 7, 8) * 8 + self.X * 4 + self.Y * 2 + self.yl}

    def barrier_signal(self, sem):
        for k in range(1, 32):
            to = device(
                self.z,
                flip(self.X, k // 16),
                flip(self.xl, k // 8 % 2),
                flip(self.Y, k // 4 % 2),
                flip(self.yl, k // 2 % 2),
                flip(self.c, k % 2),
            )
            pl.semaphore_signal(sem, inc=1, device_id=to, device_id_type=MESH)
        for to in (self.above(), self.below()):
            pl.semaphore_signal(sem, inc=1, device_id=to, device_id_type=MESH)
        for d in (self.plane(1), self.plane(7)):
            for i in range(4):
                pl.semaphore_signal(sem, inc=1, device_id=self.taker(d, i), device_id_type=MESH)
            for i in range(1, 4):
                X, Y = flip(self.xl, i // 2), flip(self.yl, i % 2)
                to = device(d, X, self.X, Y, self.Y, self.c)
                pl.semaphore_signal(sem, inc=1, device_id=to, device_id_type=MESH)


BARRIER_COUNT = 47


def device(z, X, xl, Y, yl, c):
    return {"ctx": z * 8 + X * 4 + Y * 2 + yl, "head": xl * 2 + c}


def remote(src, dst, send, recv, to):
    return pltpu.make_async_remote_copy(
        src_ref=src, dst_ref=dst, send_sem=send, recv_sem=recv, device_id=to, device_id_type=MESH
    )


def dot(a, b, contract):
    return lax.dot_general(a, b, ((contract[:1], contract[1:]), ((), ())), preferred_element_type=F32)


def terms(q, o, lse, delta, k, v, mask):
    scores = dot(k, q, (1, 1)) * (SCALE * LOG2E)
    weights = jnp.exp2(scores - lse)
    if mask is not None:
        weights = jnp.where(mask, weights, 0.0)
    slopes = weights * (dot(v, o, (1, 1)) - delta)
    return weights.astype(BF16), slopes.astype(BF16)


def kernel(
    tab,
    q_ref,
    o_ref,
    k_ref,
    v_ref,
    ld_ref,
    out_q,
    out_k,
    out_v,
    q_in,
    o_in,
    own_kv,
    ld_in,
    kvl,
    kvz_0,
    kvz_1,
    picked,
    gkv,
    gate_out,
    gate_in,
    own_out,
    own_in,
    dq_sum,
    dq_out,
    run,
    z_out,
    z_in,
    end_out,
    end_in,
    q_send,
    q_recv,
    ld_send,
    ld_recv,
    n_send,
    n_recv,
    z_send,
    z_recv,
    r_send,
    r_recv,
    b_send,
    b_recv,
    g_send,
    g_recv,
    s_send,
    s_recv,
    e_send,
    e_recv,
    l_sem,
):
    kvz = (kvz_0, kvz_1)
    me = Place()
    barrier = pltpu.get_barrier_semaphore()
    me.barrier_signal(barrier)
    for g in range(4):
        kvl[g, :, :128] = k_ref[:, g * 128 : (g + 1) * 128]
        kvl[g, :, 128:] = v_ref[:, g * 128 : (g + 1) * 128]
    for i in range(PARTS):
        run[i, 32] = jnp.zeros((PART, 256), F32)
    pl.semaphore_wait(barrier, BARRIER_COUNT)

    staying = (me.xl == me.X) & (me.yl == me.Y)
    sent = []
    maybe_sent = []

    def start(copy, here=None, local=None):
        if here is None:
            copy.start()
            sent.append(copy)
            return

        @pl.when(here)
        def _():
            local()

        @pl.when(jnp.logical_not(here))
        def _():
            copy.start()

        maybe_sent.append((here, copy))

    def await_part(part, send, recv, here=None):
        copy = remote(part, part, send, recv, me.above())
        if here is None:
            copy.wait_recv()
            return

        @pl.when(jnp.logical_not(here))
        def _():
            copy.wait_recv()

    slot = me.X * 2 + me.Y
    for i in range(PARTS):
        for n, step in enumerate((1, 7, 0)):
            for g in range(4):
                copy = remote(
                    kvl.at[g, pl.ds(i * PART, PART)],
                    kvz[i].at[me.b],
                    n_send.at[n, g, i],
                    n_recv.at[n, slot, i],
                    me.taker(me.plane(step), g),
                )
                if n == 2 and g == 0:

                    def keep():
                        kvz[i][me.b] = kvl[0, i * PART : (i + 1) * PART]

                    start(copy, staying, keep)
                else:
                    start(copy)

    for k in range(1, 8):
        to, _, e = me.inner(k)
        start(remote(kvl.at[e // 2], own_kv.at[me.s], q_send.at[2, k], q_recv.at[2, k], to))
    ld_yl = xor(me.c, me.Y)
    ld_xl = xor(me.xl, me.X)
    for core in range(2):
        to = device(me.z, me.X, ld_xl, me.Y, ld_yl, core)
        here = (ld_xl == me.xl) & (ld_yl == me.yl) & (me.c == core)

        def keep():
            ld_in[me.yl] = ld_ref[...]

        start(
            remote(ld_ref, ld_in.at[me.yl], ld_send.at[core], ld_recv.at[me.yl], to), here, keep
        )
    for k in range(1, 8):
        to, _, e = me.inner(k)
        cols = pl.ds(pl.multiple_of(e * 512, 512), 512)
        for i, (src, dst) in enumerate(((q_ref, q_in), (o_ref, o_in))):
            start(remote(src.at[:, cols], dst.at[me.s], q_send.at[i, k], q_recv.at[i, k], to))
    my_cols = pl.ds(pl.multiple_of(me.e * 512, 512), 512)
    local = [
        pltpu.make_async_copy(src.at[:, my_cols], dst.at[me.s], l_sem.at[i])
        for i, (src, dst) in enumerate(((q_ref, q_in), (o_ref, o_in)))
    ]
    for copy in local:
        copy.start()
    own_kv[me.s] = kvl[me.g]

    neighbour = (me.above(), me.below())

    def chunk(d, i, first, count):
        return kvz[i].at[pl.ds(lax.rem(d + 8, 8) * 4 + first, count)]

    def pass_on(way, t, i):
        d = me.z - t if way == 0 else me.z + t
        part = chunk(d, i, *((way * 2, 2) if t == 3 else (0, 4)))
        start(remote(part, part, z_send.at[way, t, i], z_recv.at[way, t, i], neighbour[way]))

    def arrived(way, t, i):
        d = me.z - t - 1 if way == 0 else me.z + t + 1
        part = chunk(d, i, *((way * 2, 2) if t == 3 else (0, 4)))
        await_part(part, z_send.at[way, t, i], z_recv.at[way, t, i])

    def arrived_first(n, i):
        d = (me.z + 7, me.z + 1, me.z)[n]
        for w in range(4):
            block = kvz[i].at[lax.rem(d, 8) * 4 + w]
            here = staying & (slot == w) if n == 2 else None
            await_part(block, n_send.at[n, 0, i], n_recv.at[n, w, i], here)

    for i in range(PARTS):
        for way in range(2):
            arrived_first(way, i)
            pass_on(way, 1, i)

    def pick(i):
        for k in (7, 6, 5, 4, 3, 2, 1, 0):
            to, p = me.row(k)
            for h in range(4):
                got = kvz[i][tab[0, p * 4 + h]]
                if k == 0:
                    gkv[i, me.m, h] = got
                else:
                    picked[i, k, h] = got
            if k:
                start(
                    remote(picked.at[i, k], gkv.at[i, me.m], r_send.at[i, k], r_recv.at[i, k], to)
                )

    for t in range(2, 4):
        for i in range(PARTS):
            for way in range(2):
                arrived(way, t - 1, i)
                pass_on(way, t, i)
    for i in range(PARTS):
        for way in range(2):
            arrived(way, 3, i)
        arrived_first(2, i)
        pick(i)

    for copy in local:
        copy.wait()
    for k in range(1, 8):
        _, s, _ = me.inner(k)
        for i, dst in enumerate((q_in, o_in, own_kv)):
            await_part(dst.at[s], q_send.at[i, k], q_recv.at[i, k])
    for yl in range(2):
        here = (me.gx == me.xl) & (me.gy == me.c) & (me.yl == yl)
        await_part(ld_in.at[yl], ld_send.at[0], ld_recv.at[yl], here)

    def rows_of(h):
        row = 4 * me.c + h
        lse = jnp.concatenate([ld_in[i, pl.ds(row, 1), :] for i in range(2)], axis=1) * LOG2E
        delta = jnp.concatenate([ld_in[i, pl.ds(row + 8, 1), :] for i in range(2)], axis=1)
        lanes = slice(h * 128, (h + 1) * 128)
        q = q_in[:, :, lanes].reshape(512, 128)
        o = o_in[:, :, lanes].reshape(512, 128)
        return q, o, lse, delta

    TILE = 256
    key_pos = lax.broadcasted_iota(jnp.int32, (TILE, TILE), 0)
    query_pos = lax.broadcasted_iota(jnp.int32, (TILE, TILE), 1)
    causal = key_pos <= query_pos
    own = own_kv[...].reshape(512, 256)
    own_k, own_v = own[:, :128], own[:, 128:]
    own_dk = [jnp.zeros((TILE, 128), F32) for _ in range(2)]
    own_dv = [jnp.zeros((TILE, 128), F32) for _ in range(2)]
    for h in range(4):
        q, o, lse, delta = rows_of(h)
        for i in range(2):
            cols = slice(i * TILE, (i + 1) * TILE)
            dq = jnp.zeros((TILE, 128), F32)
            for j in range(i + 1):
                keys = slice(j * TILE, (j + 1) * TILE)
                mask = causal if i == j else None
                w, s = terms(
                    q[cols], o[cols], lse[:, cols], delta[:, cols], own_k[keys], own_v[keys], mask
                )
                own_dv[j] += dot(w, o[cols], (1, 0))
                own_dk[j] += dot(s, q[cols], (1, 0))
                dq += dot(s, own_k[keys], (0, 0))
            dq_sum[h, cols] = dq
    for j in range(2):
        part = jnp.concatenate([own_dk[j] * SCALE, own_dv[j]], axis=1).astype(BF16)
        own_out[j * 4 : (j + 1) * 4] = part.reshape(4, 64, 256)
    for k in range(1, 8):
        to, s, _ = me.inner(k)
        start(remote(own_out.at[s], own_in.at[me.e], q_send.at[3, k], q_recv.at[3, k], to))
    own_in[me.e] = own_out[me.s]

    keys = 8 * PART
    for i in range(PARTS):
        for k in range(1, 8):
            _, p = me.row(k)
            await_part(gkv.at[i, p], r_send.at[i, k], r_recv.at[i, k])
        for h in range(4):
            q, o, lse, delta = rows_of(h)
            lse = jnp.where(tab[0, me.m * 4 + h] != me.b, lse, 1e30)
            kv = gkv[i, :, h].reshape(keys, 256)
            k_rows, v_rows = kv[:, :128], kv[:, 128:]
            dk = jnp.zeros((keys, 128), F32)
            dv = jnp.zeros((keys, 128), F32)
            for j in range(2):
                cols = slice(j * TILE, (j + 1) * TILE)
                w, s = terms(q[cols], o[cols], lse[:, cols], delta[:, cols], k_rows, v_rows, None)
                dv += dot(w, o[cols], (1, 0))
                dk += dot(s, q[cols], (1, 0))
                dq = dq_sum[h, cols] + dot(s, k_rows, (0, 0))
                if i < PARTS - 1:
                    dq_sum[h, cols] = dq
                else:
                    part = (dq * SCALE).astype(BF16).reshape(4, 64, 128)
                    dq_out[j * 4 : (j + 1) * 4, :, h * 128 : (h + 1) * 128] = part
            part = jnp.concatenate([dk * SCALE, dv], axis=1).astype(BF16)
            gate_out[i, :, h] = part.reshape(8, PART, 256)
        for k in (7, 6, 5, 4, 3, 2, 1):
            to, p = me.row(k)
            start(
                remote(gate_out.at[i, p], gate_in.at[i, me.m], b_send.at[i, k], b_recv.at[i, k], to)
            )
        gate_in[i, me.m] = gate_out[i, me.m]
    for k in range(1, 8):
        to, s, _ = me.inner(k)
        start(remote(dq_out.at[s], out_q.at[:, my_cols], g_send.at[k], g_recv.at[k], to))
    dq_local = pltpu.make_async_copy(dq_out.at[me.s], out_q.at[:, my_cols], l_sem.at[0])
    dq_local.start()

    def add_up(i):
        for k in range(1, 8):
            _, p = me.row(k)
            await_part(gate_in.at[i, p], b_send.at[i, k], b_recv.at[i, k])

        def add(j, carry):
            run[i, j] = gate_in[i, j // 4, lax.rem(j, 4)].astype(F32) + run[i, tab[1, j]]
            return carry

        lax.fori_loop(0, 32, add, 0)

    def total(i, d, w):
        return run[i, tab[2, lax.rem(d + 8, 8) * 4 + w]]

    def sum_on(way, t, i):
        d = me.z + 4 - t if way == 0 else me.z - 4 + t
        first = way * 2
        if t:
            part = z_in.at[way, t - 1, i]
            if t == 1:
                part = part.at[pl.ds(first, 2)]
            await_part(part, s_send.at[way, t - 1, i], s_recv.at[way, t - 1, i])
        for w in range(4):
            half = first <= w < first + 2
            if t == 0 and not half:
                continue
            value = total(i, d, w)
            if t >= 2 or (t == 1 and half):
                value += z_in[way, t - 1, i, w].astype(F32)
            z_out[way, t, i, w] = value.astype(BF16)
        if t < 3:
            src, dst = z_out.at[way, t, i], z_in.at[way, t, i]
            if t == 0:
                src, dst = src.at[pl.ds(first, 2)], dst.at[pl.ds(first, 2)]
            start(remote(src, dst, s_send.at[way, t, i], s_recv.at[way, t, i], neighbour[way]))
        else:
            for w in range(4):
                start(
                    remote(
                        z_out.at[way, t, i, w],
                        end_in.at[way, me.g, i],
                        e_send.at[way, w, i],
                        e_recv.at[way, me.g, i],
                        me.owner(lax.rem(d + 8, 8), w),
                    )
                )

    def sum_here(i):
        for w in range(4):
            end_out[i, w] = total(i, me.z, w).astype(BF16)
            copy = remote(
                end_out.at[i, w],
                end_in.at[2, me.g, i],
                e_send.at[2, w, i],
                e_recv.at[2, me.g, i],
                me.owner(me.z, w),
            )

            def keep():
                end_in[2, 0, i] = end_out[i, w]

            start(copy, staying & (slot == w), keep)

    add_up(0)
    for t in range(2):
        for way in range(2):
            sum_on(way, t, 0)
    for i in range(1, PARTS):
        add_up(i)
        for way in range(2):
            sum_on(way, 0, i)
    for t in range(1, 4):
        for i in range(PARTS):
            if i == 0 and t == 1:
                continue
            for way in range(2):
                sum_on(way, t, i)
    for i in range(PARTS):
        sum_here(i)

    for k in range(1, 8):
        _, _, e = me.inner(k)
        await_part(own_in.at[e], q_send.at[3, k], q_recv.at[3, k])
    for i in range(PARTS):
        toks = slice(i * PART, (i + 1) * PART)
        for g in range(4):
            value = own_in[2 * g, toks].astype(F32) + own_in[2 * g + 1, toks].astype(F32)
            for n in range(3):
                here = staying if n == 2 and g == 0 else None
                await_part(end_in.at[n, g, i], e_send.at[n, g, i], e_recv.at[n, g, i], here)
                value += end_in[n, g, i].astype(F32)
            out_k[toks, g * 128 : (g + 1) * 128] = value[:, :128].astype(BF16)
            out_v[toks, g * 128 : (g + 1) * 128] = value[:, 128:].astype(BF16)

    dq_local.wait()
    for k in range(1, 8):
        _, _, e = me.inner(k)
        part = out_q.at[:, pl.ds(pl.multiple_of(e * 512, 512), 512)]
        await_part(part, g_send.at[k], g_recv.at[k])
    for here, copy in maybe_sent:

        @pl.when(jnp.logical_not(here))
        def _():
            copy.wait_send()

    for copy in sent:
        copy.wait_send()


def vmem(count):
    return [pl.BlockSpec(memory_space=pltpu.VMEM)] * count


SMEM_SPEC = pl.BlockSpec(memory_space=pltpu.SMEM)
ANY_SPEC = pl.BlockSpec(memory_space=pl.ANY)
DMA = pltpu.SemaphoreType.DMA
VMEM_LIMIT = 48 * 1024 * 1024


def shape(*dims, dtype=BF16):
    return jax.ShapeDtypeStruct(dims, dtype)


def shards(queries, keys, values, out_grad, lse, delta, gate_block):
    ctx, head = lax.axis_index("ctx"), lax.axis_index("head")
    z, X, Y, yl, xl = ctx // 8, ctx // 4 % 2, ctx // 2 % 2, ctx % 2, head // 2
    g = (xl + X) % 2 * 2 + (yl + Y) % 2
    gates = lax.dynamic_slice(gate_block, (z * 4, g * 8), (4, 8)).reshape(32)
    slots = jnp.arange(32, dtype=jnp.int32)
    same = (gates[:, None] == gates[None, :]) & (slots[None, :] < slots[:, None])
    previous = jnp.max(jnp.where(same, slots[None, :], -1), axis=1)
    member = gates[None, :] == slots[:, None]
    last = jnp.max(jnp.where(member, slots[None, :], -1), axis=1)
    tab = jnp.stack([gates, jnp.where(previous < 0, 32, previous), jnp.where(last < 0, 32, last)])
    ld = jnp.concatenate([lse.T, delta.T], axis=0)

    def buf(*dims, dtype=BF16):
        return pltpu.VMEM(dims, dtype)

    return pl.pallas_call(
        kernel,
        out_shape=(shape(64, 4096), shape(64, 512), shape(64, 512)),
        in_specs=[SMEM_SPEC, ANY_SPEC, ANY_SPEC] + vmem(3),
        out_specs=(ANY_SPEC, *vmem(2)),
        scratch_shapes=[
            buf(8, 64, 512),
            buf(8, 64, 512),
            buf(8, 64, 256),
            buf(2, 16, 256, dtype=F32),
            buf(4, 64, 256),
            buf(32, PART, 256),
            buf(32, PART, 256),
            buf(PARTS, 8, 4, PART, 256),
            buf(PARTS, 8, 4, PART, 256),
            buf(PARTS, 8, 4, PART, 256),
            buf(PARTS, 8, 4, PART, 256),
            buf(8, 64, 256),
            buf(8, 64, 256),
            buf(4, 512, 128, dtype=F32),
            buf(8, 64, 512),
            buf(PARTS, 33, PART, 256, dtype=F32),
            buf(2, 4, PARTS, 4, PART, 256),
            buf(2, 4, PARTS, 4, PART, 256),
            buf(PARTS, 4, PART, 256),
            buf(3, 4, PARTS, PART, 256),
            DMA((4, 8)),
            DMA((4, 8)),
            DMA((2,)),
            DMA((2,)),
            DMA((3, 4, PARTS)),
            DMA((3, 4, PARTS)),
            DMA((2, 4, PARTS)),
            DMA((2, 4, PARTS)),
            DMA((PARTS, 8)),
            DMA((PARTS, 8)),
            DMA((PARTS, 8)),
            DMA((PARTS, 8)),
            DMA((8,)),
            DMA((8,)),
            DMA((2, 4, PARTS)),
            DMA((2, 4, PARTS)),
            DMA((3, 4, PARTS)),
            DMA((3, 4, PARTS)),
            DMA((2,)),
        ],
        compiler_params=pltpu.CompilerParams(
            collective_id=0, has_side_effects=True, vmem_limit_bytes=VMEM_LIMIT
        ),
        name="block_attention_backward",
    )(tab, queries, out_grad, keys, values, ld)


def solution(mesh):
    rows = P(("ctx", "head"), None)
    return jax.shard_map(
        shards,
        mesh=mesh,
        in_specs=(rows, rows, rows, rows, P("ctx", "head"), P("ctx", "head"), P()),
        out_specs=(rows, rows, rows),
        check_vma=False,
    )
```

time: 1000 us -> 77.9 us (0.08)
  waiting for transfers between devices: 654 us -> 0 us
  loops' own time: 167 us -> 0 us
  local copies, waits for them, and re-layouts: 101 us -> 5.08 us
  Pallas kernels: 0 us -> 70.8 us
  starting transfers between devices: 24.6 us -> 0 us
  blocking collectives: 14.7 us -> 0 us
  matrix products: 14.4 us -> 0 us
  between operations: 13.9 us -> 0.86 us
    reduce_scatter x1 -> x0, waiting for transfers between devices: 417 us -> none  [shards(): lax.psum_scatter(term.reshape(row_total, 2 * head_dim), 'ctx', scatter_di...]
    all_gather x2 -> x0, waiting for transfers between devices: 223 us -> none  [the longest x1 128 us: shards(): v_piece = lax.all_gather(v_local, 'ctx', axis=0, tiled=True)]
    another operation x289 -> x0, loops' own time: 167 us -> none  [the longest x1 162 us: shards(): lax.fori_loop(0, k_piece.shape[0] // tile_size, tile_step, empty)]
    pallas_call x0 -> x1, Pallas kernels: none -> 70.8 us  [shards(): pl.pallas_call(kernel, out_shape=(shape(64, 4096), shape(64, 512), shape(...]
    dynamic_slice x32 -> x1, local copies, waits for them, and re-layouts: 31.8 us -> 0.77 us  [shards(): gates = lax.dynamic_slice(gate_block, (z * 4, g * 8), (4, 8)).reshape(32)]
    all_to_all x5 -> x0, starting transfers between devices: 24.5 us -> none  [the longest x1 5.3 us: shards(): lax.all_to_all(queries, 'head', split_axis=1, concat_axis=0, tiled=True)]
    slice x33 -> x0, local copies, waits for them, and re-layouts: 22.6 us -> none  [the longest x32 21.9 us: tile_step(): slot_block[head + 1]]
    dot_general x1 -> x0, local copies, waits for them, and re-layouts: 19.3 us -> none  [shards(): jnp.einsum('tsq,sqrc->trc', picked.astype(jnp.float32), slot_tiles, preci...]
  transfers between devices with their start and end apart: 8 -> 0, of which waited for: 7 -> 0; matrix products, arithmetic and copies ran while one was open for 1% -> 0% of each run, Pallas kernels for 0% -> 0%
where the time goes in v2:
time: 77.9 us; the launch traced here: 76.9 us
  Pallas kernels  70.8 us (91%)
  local copies, waits for them, and re-layouts  5.08 us (7%)
  between operations  0.86 us (1%)
    pallas_call x1, Pallas kernels, shards(): pl.pallas_call(kernel, out_shape=(shape(64, 4096), shape(64, 512), shape(...  70.8 us
    unnamed x15, local copies, waits for them, and re-layouts  4.15 us

profile of v2, /device:TPU:2, one launch (start us, length us, event | category | flops | bytes accessed | tf_op | source)
XLA Modules:
  0.0 76.9 jit_solution(13495634558619558554)
XLA Ops:
  0.7 0.0 copy-start.5
  0.7 0.0 copy-start.4
  0.7 0.0 copy-start.2
  0.7 0.0 copy-start.3
  0.8 0.8 dynamic_slice.3
  1.6 0.1 eq.30
  1.6 0.1 stack_reshape.3
  1.7 0.2 select_reduce_fusion.1
  1.9 0.0 copy-done.5
  1.9 0.0 copy-done.4
  2.0 0.0 copy-done.2
  2.0 0.0 copy-done.3
  2.0 0.0 copy-start
  2.0 1.0 %copy-done = bf16[64,4096]{1,0:T(8,128)(2,1)S(1)} copy-done((bf16[64,4096]{1,0:T(8,128)(2,1)S(1)}, bf16[64,4096]{1,0:T(8,128)(2,1)}, u32[]{:S(2)}) %copy-start) | copy-done | bytes 524312
  3.0 0.0 copy-start.1
  3.0 1.0 %copy-done.1 = bf16[64,4096]{1,0:T(8,128)(2,1)S(1)} copy-done((bf16[64,4096]{1,0:T(8,128)(2,1)S(1)}, bf16[64,4096]{1,0:T(8,128)(2,1)}, u32[]{:S(2)}) %copy-start.1) | copy-done | bytes 524312
  4.1 70.8 %block_attention_backward.1 = (bf16[64,4096]{1,0:T(8,128)(2,1)S(1)}, bf16[64,512]{1,0:T(8,128)(2,1)S(1)}, bf16[64,512]{1,0:T(8,128)(2,1)S(1)}) custom-call(s32[3,32]{1,0:T(4,128)S(1)} %pad_add_fusion.tab, bf16[64,4096]{1,0:T(8,128)(2,1)S(1)} %copy-done, bf16[64,4096]{1,0:T(8,128)(2,1)S(1)} %copy-done.1, bf16[64,512]{1,0:T(8,128)(2,1)S(1)} %copy-done.2, ...), custom_call_target="tpu_custom_call" | custom-call | tf_op jit(solution)/shard_map/block_attention_backward/pallas_call | solution.py:533
  74.9 0.8 %copy.13 = bf16[64,4096]{1,0:T(8,128)(2,1)} copy(bf16[64,4096]{1,0:T(8,128)(2,1)S(1)} %get-tuple-element.10) | data formatting | bytes 1048576
  75.7 0.6 copy.14
  76.3 0.6 copy.15
  (3 shorter events, 0.0 us)
Async XLA Ops:
  0.7 1.2 %copy-start.5 = (f32[256,8]{0,1:T(8,128)S(1)}, f32[256,8]{0,1:T(8,128)}, u32[]{:S(2)}) copy-start(f32[256,8]{0,1:T(8,128)} %param.11) | copy-start | bytes 24580
  0.7 1.2 %copy-start.4 = (f32[256,8]{0,1:T(8,128)S(1)}, f32[256,8]{0,1:T(8,128)}, u32[]{:S(2)}) copy-start(f32[256,8]{0,1:T(8,128)} %param.12) | copy-start | bytes 24580
  0.7 1.2 %copy-start.2 = (bf16[64,512]{1,0:T(8,128)(2,1)S(1)}, bf16[64,512]{1,0:T(8,128)(2,1)}, u32[]{:S(2)}) copy-start(bf16[64,512]{1,0:T(8,128)(2,1)} %k_ref.1) | copy-start | bytes 196612
  0.7 1.2 %copy-start.3 = (bf16[64,512]{1,0:T(8,128)(2,1)S(1)}, bf16[64,512]{1,0:T(8,128)(2,1)}, u32[]{:S(2)}) copy-start(bf16[64,512]{1,0:T(8,128)(2,1)} %v_ref.1) | copy-start | bytes 196612
  2.0 1.0 %copy-start = (bf16[64,4096]{1,0:T(8,128)(2,1)S(1)}, bf16[64,4096]{1,0:T(8,128)(2,1)}, u32[]{:S(2)}) copy-start(bf16[64,4096]{1,0:T(8,128)(2,1)} %q_ref.1) | copy-start | bytes 1572868
  3.0 1.0 %copy-start.1 = (bf16[64,4096]{1,0:T(8,128)(2,1)S(1)}, bf16[64,4096]{1,0:T(8,128)(2,1)}, u32[]{:S(2)}) copy-start(bf16[64,4096]{1,0:T(8,128)(2,1)} %o_ref.1) | copy-start | bytes 1572868

commit v3 on v2

--- a/solution.py
+++ b/solution.py
@@ -12,7 +12,7 @@
 SCALE = 1.0 / math.sqrt(128.0)
 F32 = jnp.float32
 BF16 = jnp.bfloat16
-PARTS = 2
+PARTS = 4
 PART = 64 // PARTS
 
 
@@ -49,20 +49,15 @@
         X, Y, c = flip(self.X, k // 4), flip(self.Y, k // 2 % 2), flip(self.c, k % 2)
         return device(self.z, X, xor(self.gx, X), Y, xor(self.gy, Y), c), X * 4 + Y * 2 + c
 
+    def taker(self, step, g):
+        z = lax.rem(self.z + step + 8, 8)
+        return device(z, self.xl, xor(self.xl, g // 2), self.yl, xor(self.yl, g % 2), self.c)
+
+    def owner(self, w):
+        return device(self.z, w // 2, self.X, w % 2, self.Y, self.c)
+
     def plane(self, step):
-        return lax.rem(self.z + step, 8)
-
-    def taker(self, d, g):
-        return device(d, self.xl, xor(self.xl, g // 2), self.yl, xor(self.yl, g % 2), self.c)
-
-    def owner(self, d, w):
-        return device(d, w // 2, self.X, w % 2, self.Y, self.c)
-
-    def above(self):
-        return {"ctx": lax.rem(self.z + 1, 8) * 8 + self.X * 4 + self.Y * 2 + self.yl}
-
-    def below(self):
-        return {"ctx": lax.rem(self.z + 7, 8) * 8 + self.X * 4 + self.Y * 2 + self.yl}
+        return {"ctx": lax.rem(self.z + step + 8, 8) * 8 + self.X * 4 + self.Y * 2 + self.yl}
 
     def barrier_signal(self, sem):
         for k in range(1, 32):
@@ -75,18 +70,19 @@
                 flip(self.c, k % 2),
             )
             pl.semaphore_signal(sem, inc=1, device_id=to, device_id_type=MESH)
-        for to in (self.above(), self.below()):
-            pl.semaphore_signal(sem, inc=1, device_id=to, device_id_type=MESH)
-        for d in (self.plane(1), self.plane(7)):
+        for step in (1, -1, 2, -2):
+            pl.semaphore_signal(sem, inc=1, device_id=self.plane(step), device_id_type=MESH)
+        for step in (1, -1):
             for i in range(4):
-                pl.semaphore_signal(sem, inc=1, device_id=self.taker(d, i), device_id_type=MESH)
+                to = self.taker(step, i)
+                pl.semaphore_signal(sem, inc=1, device_id=to, device_id_type=MESH)
             for i in range(1, 4):
                 X, Y = flip(self.xl, i // 2), flip(self.yl, i % 2)
-                to = device(d, X, self.X, Y, self.Y, self.c)
+                to = device(lax.rem(self.z + step + 8, 8), X, self.X, Y, self.Y, self.c)
                 pl.semaphore_signal(sem, inc=1, device_id=to, device_id_type=MESH)
 
 
-BARRIER_COUNT = 47
+BARRIER_COUNT = 49
 
 
 def device(z, X, xl, Y, yl, c):
@@ -113,15 +109,18 @@
 
 
 def kernel(
-    tab,
+    gate_ref,
     q_ref,
     o_ref,
     k_ref,
     v_ref,
-    ld_ref,
+    l_ref,
+    d_ref,
     out_q,
     out_k,
     out_v,
+    tab,
+    ld_ref,
     q_in,
     o_in,
     own_kv,
@@ -129,6 +128,8 @@
     kvl,
     kvz_0,
     kvz_1,
+    kvz_2,
+    kvz_3,
     picked,
     gkv,
     gate_out,
@@ -162,13 +163,14 @@
     e_recv,
     l_sem,
 ):
-    kvz = (kvz_0, kvz_1)
+    kvz = (kvz_0, kvz_1, kvz_2, kvz_3)
     me = Place()
     barrier = pltpu.get_barrier_semaphore()
     me.barrier_signal(barrier)
     for g in range(4):
         kvl[g, :, :128] = k_ref[:, g * 128 : (g + 1) * 128]
         kvl[g, :, 128:] = v_ref[:, g * 128 : (g + 1) * 128]
+    ld_ref[:8], ld_ref[8:] = l_ref[...], d_ref[...]
     for i in range(PARTS):
         run[i, 32] = jnp.zeros((PART, 256), F32)
     pl.semaphore_wait(barrier, BARRIER_COUNT)
@@ -194,7 +196,7 @@
         maybe_sent.append((here, copy))
 
     def await_part(part, send, recv, here=None):
-        copy = remote(part, part, send, recv, me.above())
+        copy = remote(part, part, send, recv, me.plane(1))
         if here is None:
             copy.wait_recv()
             return
@@ -204,17 +206,18 @@
             copy.wait_recv()
 
     slot = me.X * 2 + me.Y
+    STEPS = (1, -1, 0)
     for i in range(PARTS):
-        for n, step in enumerate((1, 7, 0)):
+        for n, step in enumerate(STEPS):
             for g in range(4):
                 copy = remote(
                     kvl.at[g, pl.ds(i * PART, PART)],
                     kvz[i].at[me.b],
                     n_send.at[n, g, i],
                     n_recv.at[n, slot, i],
-                    me.taker(me.plane(step), g),
+                    me.taker(step, g),
                 )
-                if n == 2 and g == 0:
+                if step == 0 and g == 0:
 
                     def keep():
                         kvz[i][me.b] = kvl[0, i * PART : (i + 1) * PART]
@@ -252,32 +255,44 @@
         copy.start()
     own_kv[me.s] = kvl[me.g]
 
-    neighbour = (me.above(), me.below())
+    def fill(j, carry):
+        tab[0, j] = gate_ref[me.z * 4 + j // 8, me.g * 8 + lax.rem(j, 8)]
+        return carry
+
+    def link(j, carry):
+        mine = tab[0, j]
+        previous, last = jnp.int32(32), jnp.int32(32)
+        for other in range(32):
+            gate = tab[0, other]
+            previous = jnp.where((gate == mine) & (other < j), other, previous)
+            last = jnp.where(gate == j, other, last)
+        tab[1, j] = previous
+        tab[2, j] = last
+        return carry
+
+    lax.fori_loop(0, 32, fill, 0)
+    lax.fori_loop(0, 32, link, 0)
 
     def chunk(d, i, first, count):
         return kvz[i].at[pl.ds(lax.rem(d + 8, 8) * 4 + first, count)]
 
+    def span(way, t):
+        return (way * 2, 2) if t == 3 else (0, 4)
+
     def pass_on(way, t, i):
-        d = me.z - t if way == 0 else me.z + t
-        part = chunk(d, i, *((way * 2, 2) if t == 3 else (0, 4)))
-        start(remote(part, part, z_send.at[way, t, i], z_recv.at[way, t, i], neighbour[way]))
+        sign = 1 - 2 * way
+        part = chunk(me.z - sign * t, i, *span(way, t))
+        start(remote(part, part, z_send.at[way, t, i], z_recv.at[way, t, i], me.plane(sign)))
 
     def arrived(way, t, i):
-        d = me.z - t - 1 if way == 0 else me.z + t + 1
-        part = chunk(d, i, *((way * 2, 2) if t == 3 else (0, 4)))
+        part = chunk(me.z - (1 - 2 * way) * (t + 1), i, *span(way, t))
         await_part(part, z_send.at[way, t, i], z_recv.at[way, t, i])
 
     def arrived_first(n, i):
-        d = (me.z + 7, me.z + 1, me.z)[n]
         for w in range(4):
-            block = kvz[i].at[lax.rem(d, 8) * 4 + w]
+            block = kvz[i].at[lax.rem(me.z - STEPS[n] + 8, 8) * 4 + w]
             here = staying & (slot == w) if n == 2 else None
             await_part(block, n_send.at[n, 0, i], n_recv.at[n, w, i], here)
-
-    for i in range(PARTS):
-        for way in range(2):
-            arrived_first(way, i)
-            pass_on(way, 1, i)
 
     def pick(i):
         for k in (7, 6, 5, 4, 3, 2, 1, 0):
@@ -293,14 +308,21 @@
                     remote(picked.at[i, k], gkv.at[i, me.m], r_send.at[i, k], r_recv.at[i, k], to)
                 )
 
-    for t in range(2, 4):
+    def both(what, *args):
+        for way in range(2):
+            what(*args[:-2], way, *args[-2:])
+
+    for i in range(PARTS):
+        for way in range(2):
+            arrived_first(way, i)
+            pass_on(way, 1, i)
+    for t in (2, 3):
         for i in range(PARTS):
             for way in range(2):
                 arrived(way, t - 1, i)
                 pass_on(way, t, i)
     for i in range(PARTS):
-        for way in range(2):
-            arrived(way, 3, i)
+        both(arrived, 3, i)
         arrived_first(2, i)
         pick(i)
 
@@ -405,70 +427,64 @@
     def total(i, d, w):
         return run[i, tab[2, lax.rem(d + 8, 8) * 4 + w]]
 
+    HOPS = (1, 2, 1, 2)
+
     def sum_on(way, t, i):
-        d = me.z + 4 - t if way == 0 else me.z - 4 + t
-        first = way * 2
-        if t:
-            part = z_in.at[way, t - 1, i]
+        sign = 1 - 2 * way
+        first, count = span(way, t)
+        for w in range(first, first + count):
+            value = total(i, me.z + sign * (t + 1), w)
             if t == 1:
-                part = part.at[pl.ds(first, 2)]
-            await_part(part, s_send.at[way, t - 1, i], s_recv.at[way, t - 1, i])
+                value += z_in[way, 2, i, w].astype(F32)
+                if way * 2 <= w < way * 2 + 2:
+                    value += z_in[way, 3, i, w].astype(F32)
+            z_out[way, t, i, w] = value.astype(BF16)
+        src = z_out.at[way, t, i, pl.ds(first, count)]
+        dst = z_in.at[way, t, i, pl.ds(first, count)]
+        to = me.plane(sign * HOPS[t])
+        start(remote(src, dst, s_send.at[way, t, i], s_recv.at[way, t, i], to))
+
+    def sum_arrived(way, t, i):
+        part = z_in.at[way, t, i, pl.ds(*span(way, t))]
+        await_part(part, s_send.at[way, t, i], s_recv.at[way, t, i])
+
+    def middle(i):
+        for way in range(2):
+            sum_arrived(way, 2, i)
+            sum_arrived(way, 3, i)
+            sum_on(way, 1, i)
+
+    def sum_here(i):
+        for t in range(2):
+            both(sum_arrived, t, i)
         for w in range(4):
-            half = first <= w < first + 2
-            if t == 0 and not half:
-                continue
-            value = total(i, d, w)
-            if t >= 2 or (t == 1 and half):
-                value += z_in[way, t - 1, i, w].astype(F32)
-            z_out[way, t, i, w] = value.astype(BF16)
-        if t < 3:
-            src, dst = z_out.at[way, t, i], z_in.at[way, t, i]
-            if t == 0:
-                src, dst = src.at[pl.ds(first, 2)], dst.at[pl.ds(first, 2)]
-            start(remote(src, dst, s_send.at[way, t, i], s_recv.at[way, t, i], neighbour[way]))
-        else:
-            for w in range(4):
-                start(
-                    remote(
-                        z_out.at[way, t, i, w],
-                        end_in.at[way, me.g, i],
-                        e_send.at[way, w, i],
-                        e_recv.at[way, me.g, i],
-                        me.owner(lax.rem(d + 8, 8), w),
-                    )
-                )
-
-    def sum_here(i):
-        for w in range(4):
-            end_out[i, w] = total(i, me.z, w).astype(BF16)
+            value = total(i, me.z, w)
+            for way in range(2):
+                value += z_in[way, 0, i, w].astype(F32) + z_in[way, 1, i, w].astype(F32)
+            end_out[i, w] = value
             copy = remote(
                 end_out.at[i, w],
-                end_in.at[2, me.g, i],
-                e_send.at[2, w, i],
-                e_recv.at[2, me.g, i],
-                me.owner(me.z, w),
+                end_in.at[me.g, i],
+                e_send.at[w, i],
+                e_recv.at[me.g, i],
+                me.owner(w),
             )
 
             def keep():
-                end_in[2, 0, i] = end_out[i, w]
+                end_in[0, i] = end_out[i, w]
 
             start(copy, staying & (slot == w), keep)
 
-    add_up(0)
-    for t in range(2):
-        for way in range(2):
-            sum_on(way, t, 0)
-    for i in range(1, PARTS):
+    for i in range(PARTS):
         add_up(i)
-        for way in range(2):
-            sum_on(way, 0, i)
-    for t in range(1, 4):
-        for i in range(PARTS):
-            if i == 0 and t == 1:
-                continue
-            for way in range(2):
-                sum_on(way, t, i)
-    for i in range(PARTS):
+        for t in (2, 3, 0):
+            both(sum_on, t, i)
+        if i >= 1:
+            middle(i - 1)
+        if i >= 3:
+            sum_here(i - 3)
+    middle(PARTS - 1)
+    for i in range(PARTS - 3, PARTS):
         sum_here(i)
 
     for k in range(1, 8):
@@ -478,10 +494,9 @@
         toks = slice(i * PART, (i + 1) * PART)
         for g in range(4):
             value = own_in[2 * g, toks].astype(F32) + own_in[2 * g + 1, toks].astype(F32)
-            for n in range(3):
-                here = staying if n == 2 and g == 0 else None
-                await_part(end_in.at[n, g, i], e_send.at[n, g, i], e_recv.at[n, g, i], here)
-                value += end_in[n, g, i].astype(F32)
+            here = staying if g == 0 else None
+            await_part(end_in.at[g, i], e_send.at[g, i], e_recv.at[g, i], here)
+            value += end_in[g, i]
             out_k[toks, g * 128 : (g + 1) * 128] = value[:, :128].astype(BF16)
             out_v[toks, g * 128 : (g + 1) * 128] = value[:, 128:].astype(BF16)
 
@@ -500,14 +515,31 @@
         copy.wait_send()
 
 
+def hand_over(q, k, v, out_q, out_k, out_v, held_q, held_k, held_v, in_sem, out_sem):
+    jobs = []
+    for i in range(4):
+        rows = pl.ds(i * 16, 16)
+        jobs.append((q.at[rows], held_q.at[rows], out_q.at[rows]))
+    jobs += [(k, held_k, out_k), (v, held_v, out_v)]
+    arrivals = [pltpu.make_async_copy(a, b, in_sem.at[i]) for i, (a, b, _) in enumerate(jobs)]
+    leavings = [pltpu.make_async_copy(b, c, out_sem.at[i]) for i, (_, b, c) in enumerate(jobs)]
+    for copy in arrivals:
+        copy.start()
+    for arrival, leaving in zip(arrivals, leavings):
+        arrival.wait()
+        leaving.start()
+    for copy in leavings:
+        copy.wait()
+
+
 def vmem(count):
     return [pl.BlockSpec(memory_space=pltpu.VMEM)] * count
 
 
 SMEM_SPEC = pl.BlockSpec(memory_space=pltpu.SMEM)
-ANY_SPEC = pl.BlockSpec(memory_space=pl.ANY)
+HBM_SPEC = pl.BlockSpec(memory_space=pltpu.HBM)
 DMA = pltpu.SemaphoreType.DMA
-VMEM_LIMIT = 48 * 1024 * 1024
+VMEM_LIMIT = 63 * 1024 * 1024
 
 
 def shape(*dims, dtype=BF16):
@@ -515,34 +547,23 @@
 
 
 def shards(queries, keys, values, out_grad, lse, delta, gate_block):
-    ctx, head = lax.axis_index("ctx"), lax.axis_index("head")
-    z, X, Y, yl, xl = ctx // 8, ctx // 4 % 2, ctx // 2 % 2, ctx % 2, head // 2
-    g = (xl + X) % 2 * 2 + (yl + Y) % 2
-    gates = lax.dynamic_slice(gate_block, (z * 4, g * 8), (4, 8)).reshape(32)
-    slots = jnp.arange(32, dtype=jnp.int32)
-    same = (gates[:, None] == gates[None, :]) & (slots[None, :] < slots[:, None])
-    previous = jnp.max(jnp.where(same, slots[None, :], -1), axis=1)
-    member = gates[None, :] == slots[:, None]
-    last = jnp.max(jnp.where(member, slots[None, :], -1), axis=1)
-    tab = jnp.stack([gates, jnp.where(previous < 0, 32, previous), jnp.where(last < 0, 32, last)])
-    ld = jnp.concatenate([lse.T, delta.T], axis=0)
-
     def buf(*dims, dtype=BF16):
         return pltpu.VMEM(dims, dtype)
 
-    return pl.pallas_call(
+    parts = pl.pallas_call(
         kernel,
         out_shape=(shape(64, 4096), shape(64, 512), shape(64, 512)),
-        in_specs=[SMEM_SPEC, ANY_SPEC, ANY_SPEC] + vmem(3),
-        out_specs=(ANY_SPEC, *vmem(2)),
+        in_specs=[SMEM_SPEC, HBM_SPEC, HBM_SPEC] + vmem(4),
+        out_specs=(HBM_SPEC, *vmem(2)),
         scratch_shapes=[
+            pltpu.SMEM((3, 32), jnp.int32),
+            buf(16, 256, dtype=F32),
             buf(8, 64, 512),
             buf(8, 64, 512),
             buf(8, 64, 256),
             buf(2, 16, 256, dtype=F32),
             buf(4, 64, 256),
-            buf(32, PART, 256),
-            buf(32, PART, 256),
+            *[buf(32, PART, 256) for _ in range(PARTS)],
             buf(PARTS, 8, 4, PART, 256),
             buf(PARTS, 8, 4, PART, 256),
             buf(PARTS, 8, 4, PART, 256),
@@ -554,8 +575,8 @@
             buf(PARTS, 33, PART, 256, dtype=F32),
             buf(2, 4, PARTS, 4, PART, 256),
             buf(2, 4, PARTS, 4, PART, 256),
-            buf(PARTS, 4, PART, 256),
-            buf(3, 4, PARTS, PART, 256),
+            buf(PARTS, 4, PART, 256, dtype=F32),
+            buf(4, PARTS, PART, 256, dtype=F32),
             DMA((4, 8)),
             DMA((4, 8)),
             DMA((2,)),
@@ -572,15 +593,24 @@
             DMA((8,)),
             DMA((2, 4, PARTS)),
             DMA((2, 4, PARTS)),
-            DMA((3, 4, PARTS)),
-            DMA((3, 4, PARTS)),
+            DMA((4, PARTS)),
+            DMA((4, PARTS)),
             DMA((2,)),
         ],
         compiler_params=pltpu.CompilerParams(
             collective_id=0, has_side_effects=True, vmem_limit_bytes=VMEM_LIMIT
         ),
         name="block_attention_backward",
-    )(tab, queries, out_grad, keys, values, ld)
+    )(gate_block, queries, out_grad, keys, values, lse.T, delta.T)
+    return pl.pallas_call(
+        hand_over,
+        out_shape=(shape(64, 4096), shape(64, 512), shape(64, 512)),
+        in_specs=[HBM_SPEC] * 3,
+        out_specs=(HBM_SPEC,) * 3,
+        scratch_shapes=[buf(64, 4096), buf(64, 512), buf(64, 512), DMA((6,)), DMA((6,))],
+        compiler_params=pltpu.CompilerParams(vmem_limit_bytes=VMEM_LIMIT),
+        name="hand_over",
+    )(*parts)
 
 
 def solution(mesh):

time: 77.9 us -> 72.2 us (0.927); the launches traced: 76.9 us -> 72.1 us
  local copies, waits for them, and re-layouts: 5.08 us -> 0 us
    unnamed x15 -> x0, local copies, waits for them, and re-layouts: 4.15 us -> none
    pallas_call x0 -> x1, Pallas kernels: none -> 1.89 us  [shards(): pl.pallas_call(hand_over, out_shape=(shape(64, 4096), shape(64, 512), sha...]
    pallas_call x1, Pallas kernels: 70.8 us -> 69.5 us  [shards(): pl.pallas_call(kernel, out_shape=(shape(64, 4096), shape(64, 512), shape(...]
where the time goes in v3:
time: 72.2 us; the launch traced here: 72.1 us
  Pallas kernels  71.4 us (99%)
    pallas_call x1, Pallas kernels, shards(): pl.pallas_call(kernel, out_shape=(shape(64, 4096), shape(64, 512), shape(...  69.5 us
    pallas_call x1, Pallas kernels, shards(): pl.pallas_call(hand_over, out_shape=(shape(64, 4096), shape(64, 512), sha...  1.89 us

profile of v3, /device:TPU:2, one launch (start us, length us, event | category | flops | bytes accessed | tf_op | source)
XLA Modules:
  0.0 72.1 jit_solution(1758119512535366038)
XLA Ops:
  0.6 69.5 %block_attention_backward.1 = (bf16[64,4096]{1,0:T(8,128)(2,1)}, bf16[64,512]{1,0:T(8,128)(2,1)}, bf16[64,512]{1,0:T(8,128)(2,1)}) custom-call(s32[32,32]{1,0:T(8,128)} %gate_ref.1, bf16[64,4096]{1,0:T(8,128)(2,1)} %q_ref.1, bf16[64,4096]{1,0:T(8,128)(2,1)} %o_ref.1, bf16[64,512]{1,0:T(8,128)(2,1)} %k_ref.1, bf16[64,512]{1,0:T(8,128)(2,1)} %v_ref.1, ...), custom_call_target="tpu_custom_call" | custom-call | tf_op jit(solution)/shard_map/block_attention_backward/pallas_call | solution.py:553
  70.2 1.9 %hand_over.1 = (bf16[64,4096]{1,0:T(8,128)(2,1)}, bf16[64,512]{1,0:T(8,128)(2,1)}, bf16[64,512]{1,0:T(8,128)(2,1)}) custom-call(bf16[64,4096]{1,0:T(8,128)(2,1)} %get-tuple-element.6.q, bf16[64,512]{1,0:T(8,128)(2,1)} %get-tuple-element.7.k, bf16[64,512]{1,0:T(8,128)(2,1)} %get-tuple-element.8.v), custom_call_target="tpu_custom_call" | custom-call | tf_op jit(solution)/shard_map/hand_over/pallas_call | solution.py:605

commit v4 on v3

--- a/solution.py
+++ b/solution.py
@@ -14,6 +14,8 @@
 BF16 = jnp.bfloat16
 PARTS = 4
 PART = 64 // PARTS
+GROUPS = ((0,), (1,), (2, 3))
+HALF = 32
 
 
 def flip(bit, by):
@@ -53,8 +55,8 @@
         z = lax.rem(self.z + step + 8, 8)
         return device(z, self.xl, xor(self.xl, g // 2), self.yl, xor(self.yl, g % 2), self.c)
 
-    def owner(self, w):
-        return device(self.z, w // 2, self.X, w % 2, self.Y, self.c)
+    def owner(self, w, step=0):
+        return device(lax.rem(self.z + step + 8, 8), w // 2, self.X, w % 2, self.Y, self.c)
 
     def plane(self, step):
         return {"ctx": lax.rem(self.z + step + 8, 8) * 8 + self.X * 4 + self.Y * 2 + self.yl}
@@ -72,7 +74,7 @@
             pl.semaphore_signal(sem, inc=1, device_id=to, device_id_type=MESH)
         for step in (1, -1, 2, -2):
             pl.semaphore_signal(sem, inc=1, device_id=self.plane(step), device_id_type=MESH)
-        for step in (1, -1):
+        for step in (1, -1, 2, -2):
             for i in range(4):
                 to = self.taker(step, i)
                 pl.semaphore_signal(sem, inc=1, device_id=to, device_id_type=MESH)
@@ -82,7 +84,7 @@
                 pl.semaphore_signal(sem, inc=1, device_id=to, device_id_type=MESH)
 
 
-BARRIER_COUNT = 49
+BARRIER_COUNT = 63
 
 
 def device(z, X, xl, Y, yl, c):
@@ -109,18 +111,23 @@
 
 
 def kernel(
-    gate_ref,
+    gate_hbm,
     q_ref,
     o_ref,
-    k_ref,
-    v_ref,
-    l_ref,
-    d_ref,
+    k_hbm,
+    v_hbm,
+    l_hbm,
+    d_hbm,
     out_q,
     out_k,
     out_v,
+    gate_ref,
     tab,
+    k_ref,
+    v_ref,
     ld_ref,
+    sum_k,
+    sum_v,
     q_in,
     o_in,
     own_kv,
@@ -128,8 +135,6 @@
     kvl,
     kvz_0,
     kvz_1,
-    kvz_2,
-    kvz_3,
     picked,
     gkv,
     gate_out,
@@ -143,6 +148,7 @@
     z_in,
     end_out,
     end_in,
+    far_in,
     q_send,
     q_recv,
     ld_send,
@@ -161,18 +167,28 @@
     s_recv,
     e_send,
     e_recv,
+    f_send,
+    f_recv,
     l_sem,
+    i_sem,
+    o_sem,
 ):
-    kvz = (kvz_0, kvz_1, kvz_2, kvz_3)
+    kvz = (kvz_0, kvz_1)
     me = Place()
+    first = ((k_hbm, k_ref), (v_hbm, v_ref), (gate_hbm, gate_ref))
+    first += ((l_hbm, ld_ref.at[pl.ds(0, 8)]), (d_hbm, ld_ref.at[pl.ds(8, 8)]))
+    first = [pltpu.make_async_copy(a, b, i_sem.at[n]) for n, (a, b) in enumerate(first)]
+    for copy in first:
+        copy.start()
     barrier = pltpu.get_barrier_semaphore()
     me.barrier_signal(barrier)
+    for i in range(PARTS):
+        run[i, 32] = jnp.zeros((PART, 256), F32)
+    for copy in first:
+        copy.wait()
     for g in range(4):
         kvl[g, :, :128] = k_ref[:, g * 128 : (g + 1) * 128]
         kvl[g, :, 128:] = v_ref[:, g * 128 : (g + 1) * 128]
-    ld_ref[:8], ld_ref[8:] = l_ref[...], d_ref[...]
-    for i in range(PARTS):
-        run[i, 32] = jnp.zeros((PART, 256), F32)
     pl.semaphore_wait(barrier, BARRIER_COUNT)
 
     staying = (me.xl == me.X) & (me.yl == me.Y)
@@ -207,11 +223,11 @@
 
     slot = me.X * 2 + me.Y
     STEPS = (1, -1, 0)
-    for i in range(PARTS):
+    for i in range(2):
         for n, step in enumerate(STEPS):
             for g in range(4):
                 copy = remote(
-                    kvl.at[g, pl.ds(i * PART, PART)],
+                    kvl.at[g, pl.ds(i * HALF, HALF)],
                     kvz[i].at[me.b],
                     n_send.at[n, g, i],
                     n_recv.at[n, slot, i],
@@ -220,7 +236,7 @@
                 if step == 0 and g == 0:
 
                     def keep():
-                        kvz[i][me.b] = kvl[0, i * PART : (i + 1) * PART]
+                        kvz[i][me.b] = kvl[0, i * HALF : (i + 1) * HALF]
 
                     start(copy, staying, keep)
                 else:
@@ -298,7 +314,7 @@
         for k in (7, 6, 5, 4, 3, 2, 1, 0):
             to, p = me.row(k)
             for h in range(4):
-                got = kvz[i][tab[0, p * 4 + h]]
+                got = kvz[i // 2][tab[0, p * 4 + h], i % 2 * PART : (i % 2 + 1) * PART]
                 if k == 0:
                     gkv[i, me.m, h] = got
                 else:
@@ -312,19 +328,20 @@
         for way in range(2):
             what(*args[:-2], way, *args[-2:])
 
-    for i in range(PARTS):
+    for i in range(2):
         for way in range(2):
             arrived_first(way, i)
             pass_on(way, 1, i)
     for t in (2, 3):
-        for i in range(PARTS):
+        for i in range(2):
             for way in range(2):
                 arrived(way, t - 1, i)
                 pass_on(way, t, i)
-    for i in range(PARTS):
+    for i in range(2):
+        arrived_first(2, i)
         both(arrived, 3, i)
-        arrived_first(2, i)
-        pick(i)
+        pick(2 * i)
+        pick(2 * i + 1)
 
     for copy in local:
         copy.wait()
@@ -377,36 +394,39 @@
     own_in[me.e] = own_out[me.s]
 
     keys = 8 * PART
-    for i in range(PARTS):
-        for k in range(1, 8):
-            _, p = me.row(k)
-            await_part(gkv.at[i, p], r_send.at[i, k], r_recv.at[i, k])
+    for group in GROUPS:
+        for part in group:
+            for k in range(1, 8):
+                _, p = me.row(k)
+                await_part(gkv.at[part, p], r_send.at[part, k], r_recv.at[part, k])
         for h in range(4):
             q, o, lse, delta = rows_of(h)
             lse = jnp.where(tab[0, me.m * 4 + h] != me.b, lse, 1e30)
-            kv = gkv[i, :, h].reshape(keys, 256)
+            kv = [gkv[part, :, h].reshape(keys, 256) for part in group]
+            kv = kv[0] if len(kv) == 1 else jnp.concatenate(kv, axis=0)
             k_rows, v_rows = kv[:, :128], kv[:, 128:]
-            dk = jnp.zeros((keys, 128), F32)
-            dv = jnp.zeros((keys, 128), F32)
+            dk = jnp.zeros((len(group) * keys, 128), F32)
+            dv = jnp.zeros((len(group) * keys, 128), F32)
             for j in range(2):
                 cols = slice(j * TILE, (j + 1) * TILE)
                 w, s = terms(q[cols], o[cols], lse[:, cols], delta[:, cols], k_rows, v_rows, None)
                 dv += dot(w, o[cols], (1, 0))
                 dk += dot(s, q[cols], (1, 0))
                 dq = dq_sum[h, cols] + dot(s, k_rows, (0, 0))
-                if i < PARTS - 1:
+                if group[-1] < PARTS - 1:
                     dq_sum[h, cols] = dq
                 else:
-                    part = (dq * SCALE).astype(BF16).reshape(4, 64, 128)
-                    dq_out[j * 4 : (j + 1) * 4, :, h * 128 : (h + 1) * 128] = part
-            part = jnp.concatenate([dk * SCALE, dv], axis=1).astype(BF16)
-            gate_out[i, :, h] = part.reshape(8, PART, 256)
-        for k in (7, 6, 5, 4, 3, 2, 1):
-            to, p = me.row(k)
-            start(
-                remote(gate_out.at[i, p], gate_in.at[i, me.m], b_send.at[i, k], b_recv.at[i, k], to)
-            )
-        gate_in[i, me.m] = gate_out[i, me.m]
+                    piece = (dq * SCALE).astype(BF16).reshape(4, 64, 128)
+                    dq_out[j * 4 : (j + 1) * 4, :, h * 128 : (h + 1) * 128] = piece
+            both_k_v = jnp.concatenate([dk * SCALE, dv], axis=1).astype(BF16)
+            for n, part in enumerate(group):
+                gate_out[part, :, h] = both_k_v[n * keys : (n + 1) * keys].reshape(8, PART, 256)
+        for part in group:
+            for k in (7, 6, 5, 4, 3, 2, 1):
+                to, p = me.row(k)
+                src, dst = gate_out.at[part, p], gate_in.at[part, me.m]
+                start(remote(src, dst, b_send.at[part, k], b_recv.at[part, k], to))
+            gate_in[part, me.m] = gate_out[part, me.m]
     for k in range(1, 8):
         to, s, _ = me.inner(k)
         start(remote(dq_out.at[s], out_q.at[:, my_cols], g_send.at[k], g_recv.at[k], to))
@@ -439,6 +459,14 @@
                 if way * 2 <= w < way * 2 + 2:
                     value += z_in[way, 3, i, w].astype(F32)
             z_out[way, t, i, w] = value.astype(BF16)
+        if t < 2 and i == PARTS - 1:
+            for w in range(4):
+                dst = far_in.at[way, t, me.g]
+                to = me.owner(w, sign * HOPS[t])
+                start(
+                    remote(z_out.at[way, t, i, w], dst, f_send.at[way, t, w], f_recv.at[way, t, me.g], to)
+                )
+            return
         src = z_out.at[way, t, i, pl.ds(first, count)]
         dst = z_in.at[way, t, i, pl.ds(first, count)]
         to = me.plane(sign * HOPS[t])
@@ -455,11 +483,12 @@
             sum_on(way, 1, i)
 
     def sum_here(i):
-        for t in range(2):
+        far = i == PARTS - 1
+        for t in range(0 if far else 2):
             both(sum_arrived, t, i)
         for w in range(4):
             value = total(i, me.z, w)
-            for way in range(2):
+            for way in range(0 if far else 2):
                 value += z_in[way, 0, i, w].astype(F32) + z_in[way, 1, i, w].astype(F32)
             end_out[i, w] = value
             copy = remote(
@@ -483,13 +512,15 @@
             middle(i - 1)
         if i >= 3:
             sum_here(i - 3)
+    sum_here(PARTS - 1)
+    sum_here(PARTS - 3)
     middle(PARTS - 1)
-    for i in range(PARTS - 3, PARTS):
-        sum_here(i)
+    sum_here(PARTS - 2)
 
     for k in range(1, 8):
         _, _, e = me.inner(k)
         await_part(own_in.at[e], q_send.at[3, k], q_recv.at[3, k])
+    results = []
     for i in range(PARTS):
         toks = slice(i * PART, (i + 1) * PART)
         for g in range(4):
@@ -497,10 +528,21 @@
             here = staying if g == 0 else None
             await_part(end_in.at[g, i], e_send.at[g, i], e_recv.at[g, i], here)
             value += end_in[g, i]
-            out_k[toks, g * 128 : (g + 1) * 128] = value[:, :128].astype(BF16)
-            out_v[toks, g * 128 : (g + 1) * 128] = value[:, 128:].astype(BF16)
-
-    dq_local.wait()
+            if i == PARTS - 1:
+                for way in range(2):
+                    for t in range(2):
+                        part = far_in.at[way, t, g]
+                        await_part(part, f_send.at[way, t, g], f_recv.at[way, t, g])
+                        value += far_in[way, t, g].astype(F32)
+            sum_k[toks, g * 128 : (g + 1) * 128] = value[:, :128].astype(BF16)
+            sum_v[toks, g * 128 : (g + 1) * 128] = value[:, 128:].astype(BF16)
+        for n, (src, dst) in enumerate(((sum_k, out_k), (sum_v, out_v))):
+            rows = pl.ds(i * PART, PART)
+            results.append(pltpu.make_async_copy(src.at[rows], dst.at[rows], o_sem.at[n, i]))
+            results[-1].start()
+
+    for copy in [dq_local] + results:
+        copy.wait()
     for k in range(1, 8):
         _, _, e = me.inner(k)
         part = out_q.at[:, pl.ds(pl.multiple_of(e * 512, 512), 512)]
@@ -532,11 +574,6 @@
         copy.wait()
 
 
-def vmem(count):
-    return [pl.BlockSpec(memory_space=pltpu.VMEM)] * count
-
-
-SMEM_SPEC = pl.BlockSpec(memory_space=pltpu.SMEM)
 HBM_SPEC = pl.BlockSpec(memory_space=pltpu.HBM)
 DMA = pltpu.SemaphoreType.DMA
 VMEM_LIMIT = 63 * 1024 * 1024
@@ -553,17 +590,23 @@
     parts = pl.pallas_call(
         kernel,
         out_shape=(shape(64, 4096), shape(64, 512), shape(64, 512)),
-        in_specs=[SMEM_SPEC, HBM_SPEC, HBM_SPEC] + vmem(4),
-        out_specs=(HBM_SPEC, *vmem(2)),
+        in_specs=[HBM_SPEC] * 7,
+        out_specs=(HBM_SPEC,) * 3,
         scratch_shapes=[
+            pltpu.SMEM((32, 32), jnp.int32),
             pltpu.SMEM((3, 32), jnp.int32),
+            buf(64, 512),
+            buf(64, 512),
             buf(16, 256, dtype=F32),
+            buf(64, 512),
+            buf(64, 512),
             buf(8, 64, 512),
             buf(8, 64, 512),
             buf(8, 64, 256),
             buf(2, 16, 256, dtype=F32),
             buf(4, 64, 256),
-            *[buf(32, PART, 256) for _ in range(PARTS)],
+            buf(32, HALF, 256),
+            buf(32, HALF, 256),
             buf(PARTS, 8, 4, PART, 256),
             buf(PARTS, 8, 4, PART, 256),
             buf(PARTS, 8, 4, PART, 256),
@@ -577,14 +620,15 @@
             buf(2, 4, PARTS, 4, PART, 256),
             buf(PARTS, 4, PART, 256, dtype=F32),
             buf(4, PARTS, PART, 256, dtype=F32),
+            buf(2, 2, 4, PART, 256),
             DMA((4, 8)),
             DMA((4, 8)),
             DMA((2,)),
             DMA((2,)),
-            DMA((3, 4, PARTS)),
-            DMA((3, 4, PARTS)),
-            DMA((2, 4, PARTS)),
-            DMA((2, 4, PARTS)),
+            DMA((3, 4, 2)),
+            DMA((3, 4, 2)),
+            DMA((2, 4, 2)),
+            DMA((2, 4, 2)),
             DMA((PARTS, 8)),
             DMA((PARTS, 8)),
             DMA((PARTS, 8)),
@@ -595,7 +639,11 @@
             DMA((2, 4, PARTS)),
             DMA((4, PARTS)),
             DMA((4, PARTS)),
+            DMA((2, 2, 4)),
+            DMA((2, 2, 4)),
             DMA((2,)),
+            DMA((5,)),
+            DMA((2, PARTS)),
         ],
         compiler_params=pltpu.CompilerParams(
             collective_id=0, has_side_effects=True, vmem_limit_bytes=VMEM_LIMIT

time: 72.2 us -> 70.5 us (0.976)
  Pallas kernels: 71.4 us -> 69.7 us
    pallas_call x1, Pallas kernels: 69.5 us -> 67.8 us  [shards(): pl.pallas_call(kernel, out_shape=(shape(64, 4096), shape(64, 512), shape(...]
where the time goes in v4:
time: 70.5 us; the launch traced here: 70.3 us
  Pallas kernels  69.7 us (99%)
    pallas_call x1, Pallas kernels, shards(): pl.pallas_call(kernel, out_shape=(shape(64, 4096), shape(64, 512), shape(...  67.8 us
    pallas_call x1, Pallas kernels, shards(): pl.pallas_call(hand_over, out_shape=(shape(64, 4096), shape(64, 512), sha...  1.89 us

profile of v4, /device:TPU:2, one launch (start us, length us, event | category | flops | bytes accessed | tf_op | source)
XLA Modules:
  0.0 70.3 jit_solution(15940128752093968979)
XLA Ops:
  0.6 67.8 %block_attention_backward.1 = (bf16[64,4096]{1,0:T(8,128)(2,1)}, bf16[64,512]{1,0:T(8,128)(2,1)}, bf16[64,512]{1,0:T(8,128)(2,1)}) custom-call(s32[32,32]{1,0:T(8,128)} %gate_hbm.1, bf16[64,4096]{1,0:T(8,128)(2,1)} %q_ref.1, bf16[64,4096]{1,0:T(8,128)(2,1)} %o_ref.1, bf16[64,512]{1,0:T(8,128)(2,1)} %k_hbm.1, bf16[64,512]{1,0:T(8,128)(2,1)} %v_hbm.1, ...), custom_call_target="tpu_custom_call" | custom-call | tf_op jit(solution)/shard_map/block_attention_backward/pallas_call | solution.py:590
  68.4 1.9 %hand_over.1 = (bf16[64,4096]{1,0:T(8,128)(2,1)}, bf16[64,512]{1,0:T(8,128)(2,1)}, bf16[64,512]{1,0:T(8,128)(2,1)}) custom-call(bf16[64,4096]{1,0:T(8,128)(2,1)} %get-tuple-element.6.q, bf16[64,512]{1,0:T(8,128)(2,1)} %get-tuple-element.7.k, bf16[64,512]{1,0:T(8,128)(2,1)} %get-tuple-element.8.v), custom_call_target="tpu_custom_call" | custom-call | tf_op jit(solution)/shard_map/hand_over/pallas_call | solution.py:653

commit v5 on v4

--- a/solution.py
+++ b/solution.py
@@ -61,30 +61,32 @@
     def plane(self, step):
         return {"ctx": lax.rem(self.z + step + 8, 8) * 8 + self.X * 4 + self.Y * 2 + self.yl}
 
-    def barrier_signal(self, sem):
-        for k in range(1, 32):
-            to = device(
-                self.z,
-                flip(self.X, k // 16),
-                flip(self.xl, k // 8 % 2),
-                flip(self.Y, k // 4 % 2),
-                flip(self.yl, k // 2 % 2),
-                flip(self.c, k % 2),
-            )
+    def barrier(self):
+        sem = pltpu.get_barrier_semaphore()
+
+        def greet(to):
             pl.semaphore_signal(sem, inc=1, device_id=to, device_id_type=MESH)
-        for step in (1, -1, 2, -2):
-            pl.semaphore_signal(sem, inc=1, device_id=self.plane(step), device_id_type=MESH)
-        for step in (1, -1, 2, -2):
-            for i in range(4):
-                to = self.taker(step, i)
-                pl.semaphore_signal(sem, inc=1, device_id=to, device_id_type=MESH)
+
+        for step in (2, -2, 1, -1, 0):
+            z = lax.rem(self.z + step + 8, 8)
             for i in range(1, 4):
-                X, Y = flip(self.xl, i // 2), flip(self.yl, i % 2)
-                to = device(lax.rem(self.z + step + 8, 8), X, self.X, Y, self.Y, self.c)
-                pl.semaphore_signal(sem, inc=1, device_id=to, device_id_type=MESH)
-
-
-BARRIER_COUNT = 63
+                greet(device(z, self.xl, flip(self.X, i // 2), self.yl, flip(self.Y, i % 2), self.c))
+                greet(device(z, flip(self.xl, i // 2), self.X, flip(self.yl, i % 2), self.Y, self.c))
+            if step:
+                greet(device(z, self.xl, self.X, self.yl, self.Y, self.c))
+                greet(self.plane(step))
+        for k in range(2, 8):
+            greet(self.row(k)[0])
+        for k in range(1, 8):
+            greet(self.inner(k)[0])
+        swapped = device(self.z, self.xl, self.X, self.yl, self.Y, self.c)
+        here = (self.xl == self.X) & (self.yl == self.Y)
+
+        @pl.when(jnp.logical_not(here))
+        def _():
+            greet(swapped)
+
+        return lambda: pl.semaphore_wait(sem, 52 - here.astype(jnp.int32))
 
 
 def device(z, X, xl, Y, yl, c):
@@ -180,8 +182,7 @@
     first = [pltpu.make_async_copy(a, b, i_sem.at[n]) for n, (a, b) in enumerate(first)]
     for copy in first:
         copy.start()
-    barrier = pltpu.get_barrier_semaphore()
-    me.barrier_signal(barrier)
+    everyone_is_here = me.barrier()
     for i in range(PARTS):
         run[i, 32] = jnp.zeros((PART, 256), F32)
     for copy in first:
@@ -189,7 +190,7 @@
     for g in range(4):
         kvl[g, :, :128] = k_ref[:, g * 128 : (g + 1) * 128]
         kvl[g, :, 128:] = v_ref[:, g * 128 : (g + 1) * 128]
-    pl.semaphore_wait(barrier, BARRIER_COUNT)
+    everyone_is_here()
 
     staying = (me.xl == me.X) & (me.yl == me.Y)
     sent = []
@@ -287,7 +288,6 @@
         return carry
 
     lax.fori_loop(0, 32, fill, 0)
-    lax.fori_loop(0, 32, link, 0)
 
     def chunk(d, i, first, count):
         return kvz[i].at[pl.ds(lax.rem(d + 8, 8) * 4 + first, count)]
@@ -342,6 +342,7 @@
         both(arrived, 3, i)
         pick(2 * i)
         pick(2 * i + 1)
+    lax.fori_loop(0, 32, link, 0)
 
     for copy in local:
         copy.wait()

time: 70.5 us -> 69.8 us (0.990)
  Pallas kernels: 69.7 us -> 68.9 us
    pallas_call x1, Pallas kernels: 67.8 us -> 67 us  [shards(): pl.pallas_call(kernel, out_shape=(shape(64, 4096), shape(64, 512), shape(...]
where the time goes in v5:
time: 69.8 us; the launch traced here: 69.5 us
  Pallas kernels  68.9 us (99%)
    pallas_call x1, Pallas kernels, shards(): pl.pallas_call(kernel, out_shape=(shape(64, 4096), shape(64, 512), shape(...  67 us
    pallas_call x1, Pallas kernels, shards(): pl.pallas_call(hand_over, out_shape=(shape(64, 4096), shape(64, 512), sha...  1.89 us

profile of v5, /device:TPU:2, one launch (start us, length us, event | category | flops | bytes accessed | tf_op | source)
XLA Modules:
  0.0 69.5 jit_solution(17196631331318633192)
XLA Ops:
  0.6 67.0 %block_attention_backward.1 = (bf16[64,4096]{1,0:T(8,128)(2,1)}, bf16[64,512]{1,0:T(8,128)(2,1)}, bf16[64,512]{1,0:T(8,128)(2,1)}) custom-call(s32[32,32]{1,0:T(8,128)} %gate_hbm.1, bf16[64,4096]{1,0:T(8,128)(2,1)} %q_ref.1, bf16[64,4096]{1,0:T(8,128)(2,1)} %o_ref.1, bf16[64,512]{1,0:T(8,128)(2,1)} %k_hbm.1, bf16[64,512]{1,0:T(8,128)(2,1)} %v_hbm.1, ...), custom_call_target="tpu_custom_call" | custom-call | tf_op jit(solution)/shard_map/block_attention_backward/pallas_call | solution.py:591
  67.7 1.9 %hand_over.1 = (bf16[64,4096]{1,0:T(8,128)(2,1)}, bf16[64,512]{1,0:T(8,128)(2,1)}, bf16[64,512]{1,0:T(8,128)(2,1)}) custom-call(bf16[64,4096]{1,0:T(8,128)(2,1)} %get-tuple-element.6.q, bf16[64,512]{1,0:T(8,128)(2,1)} %get-tuple-element.7.k, bf16[64,512]{1,0:T(8,128)(2,1)} %get-tuple-element.8.v), custom_call_target="tpu_custom_call" | custom-call | tf_op jit(solution)/shard_map/hand_over/pallas_call | solution.py:654

commit v6 on v5

--- a/solution.py
+++ b/solution.py
@@ -258,7 +258,7 @@
         start(
             remote(ld_ref, ld_in.at[me.yl], ld_send.at[core], ld_recv.at[me.yl], to), here, keep
         )
-    for k in range(1, 8):
+    for k in range(7, 0, -1):
         to, _, e = me.inner(k)
         cols = pl.ds(pl.multiple_of(e * 512, 512), 512)
         for i, (src, dst) in enumerate(((q_ref, q_in), (o_ref, o_in))):
@@ -507,7 +507,7 @@
 
     for i in range(PARTS):
         add_up(i)
-        for t in (2, 3, 0):
+        for t in (3, 2, 0):
             both(sum_on, t, i)
         if i >= 1:
             middle(i - 1)

time: 69.8 us -> 69.6 us (level)
  no operation moved by 1% of the time
where the time goes in v6:
time: 69.6 us; the launch traced here: 69.5 us
  Pallas kernels  68.8 us (99%)
    pallas_call x1, Pallas kernels, shards(): pl.pallas_call(kernel, out_shape=(shape(64, 4096), shape(64, 512), shape(...  66.9 us
    pallas_call x1, Pallas kernels, shards(): pl.pallas_call(hand_over, out_shape=(shape(64, 4096), shape(64, 512), sha...  1.89 us

profile of v6, /device:TPU:2, one launch (start us, length us, event | category | flops | bytes accessed | tf_op | source)
XLA Modules:
  0.0 69.5 jit_solution(9786580004851873510)
XLA Ops:
  0.6 66.9 %block_attention_backward.1 = (bf16[64,4096]{1,0:T(8,128)(2,1)}, bf16[64,512]{1,0:T(8,128)(2,1)}, bf16[64,512]{1,0:T(8,128)(2,1)}) custom-call(s32[32,32]{1,0:T(8,128)} %gate_hbm.1, bf16[64,4096]{1,0:T(8,128)(2,1)} %q_ref.1, bf16[64,4096]{1,0:T(8,128)(2,1)} %o_ref.1, bf16[64,512]{1,0:T(8,128)(2,1)} %k_hbm.1, bf16[64,512]{1,0:T(8,128)(2,1)} %v_hbm.1, ...), custom_call_target="tpu_custom_call" | custom-call | tf_op jit(solution)/shard_map/block_attention_backward/pallas_call | solution.py:591
  67.6 1.9 %hand_over.1 = (bf16[64,4096]{1,0:T(8,128)(2,1)}, bf16[64,512]{1,0:T(8,128)(2,1)}, bf16[64,512]{1,0:T(8,128)(2,1)}) custom-call(bf16[64,4096]{1,0:T(8,128)(2,1)} %get-tuple-element.6.q, bf16[64,512]{1,0:T(8,128)(2,1)} %get-tuple-element.7.k, bf16[64,512]{1,0:T(8,128)(2,1)} %get-tuple-element.8.v), custom_call_target="tpu_custom_call" | custom-call | tf_op jit(solution)/shard_map/hand_over/pallas_call | solution.py:654
